TPU v7x, 32 devices: a whole 2x2x4 slice. The times are simulated.
32 devices in a mesh: fsdp: 16 (over z, x, core), seq: 2 (over y).
Axes of the slice: x: 2, y: 2, z: 4, core: 2. Of those that a mesh axis runs over, the one named last changes fastest.
Arguments:
- latents: bfloat16 [16, 1024, 1024], P('fsdp', 'seq'), may hold values from -6 to 6
- cond: bfloat16 [16, 1024], P('fsdp'), may hold values from -6 to 6
- cotangent: bfloat16 [16, 1024, 1024], P('fsdp', 'seq'), may hold values from -6 to 6
- w_qkv: bfloat16 [1024, 3072], P('fsdp'), may hold values from -0.1875 to 0.1875
- w_out: bfloat16 [1024, 1024], P('fsdp'), may hold values from -4 to 4
- w_up: bfloat16 [1024, 4096], P('fsdp', 'seq'), may hold values from -0.1875 to 0.1875
- w_down: bfloat16 [4096, 1024], P('seq', 'fsdp'), may hold values from -0.09375 to 0.09375
- w_ada: bfloat16 [1024, 6144], P(None, 'fsdp'), may hold values from -0.1875 to 0.1875
- b_ada: bfloat16 [6144], P('fsdp'), may hold values from -3 to 3
Outputs:
- mixed: bfloat16 [16, 1024, 1024], P('fsdp', 'seq')
- grad_latents: float32 [16, 1024, 1024], P('fsdp', 'seq')
- grad_cond: float32 [16, 1024], P('fsdp')
- grad_w_qkv: float32 [1024, 3072], P('fsdp')
- grad_w_out: float32 [1024, 1024], P('fsdp')
- grad_w_up: float32 [1024, 4096], P('fsdp', 'seq')
- grad_w_down: float32 [4096, 1024], P('seq', 'fsdp')
- grad_w_ada: float32 [1024, 6144], P(None, 'fsdp')
- grad_b_ada: float32 [6144], P('fsdp')
All inputs are finite; a program needn't handle non-finite values.
Results may differ from a plain program's by a relative error of at most 0.015.
The roundings to bfloat16 on the way count: a program that leaves them out, or rounds other values in their place, can miss the bound.
Values may be sent and summed in bfloat16 or wider, within the bound.
No kernel may reach another device: no remote copies, remote signals or barrier semaphores. Data moves between devices by JAX's collectives and lax.ppermute only.
A program may use at most 128 MiB of HBM per device.

v0:
```python
from functools import partial

import jax
import jax.numpy as jnp
from jax import lax
from jax.sharding import PartitionSpec as P

H = 16
HD = 64


EPSILON = 1e-06


def normalize(value_rows):
    center = value_rows - jnp.mean(value_rows, -1, keepdims=True)
    inverse = lax.rsqrt(jnp.mean(center * center, -1, keepdims=True) + EPSILON)
    return (center * inverse, inverse)


def norm_grad(normed, inverse, grad_normed):
    return inverse * (
        grad_normed
        - jnp.mean(grad_normed, -1, keepdims=True)
        - normed * jnp.mean(grad_normed * normed, -1, keepdims=True)
    )


def split_block(head_block):
    head_depth = head_block.shape[-1] // 3
    return (
        head_block[..., :head_depth],
        head_block[..., head_depth : 2 * head_depth],
        head_block[..., 2 * head_depth :],
    )


def head_forward(head_block):
    query_rows_all, key_tile_block, value_rows = split_block(head_block)
    scores = jnp.einsum(
        "cog,cmg->com", query_rows_all, key_tile_block, preferred_element_type=jnp.float32
    ) * query_rows_all.shape[-1] ** (-0.5)
    highest = jnp.max(scores, -1, keepdims=True)
    raised = jnp.exp(scores - highest)
    totals = jnp.sum(raised, -1, keepdims=True)
    weight_matrices = (raised / totals).astype(jnp.bfloat16)
    attention_result = jnp.einsum(
        "eap,epj->eaj", weight_matrices, value_rows, preferred_element_type=jnp.float32
    )
    return (attention_result.astype(jnp.bfloat16), (highest + jnp.log(totals))[..., 0])


def head_backward(head_items):
    head_block, logsum, output_gradient = head_items
    query_rows_all, key_tile_block, value_rows = split_block(head_block)
    scaling_multiplier = query_rows_all.shape[-1] ** (-0.5)
    scores = (
        jnp.einsum(
            "cog,cmg->com", query_rows_all, key_tile_block, preferred_element_type=jnp.float32
        )
        * scaling_multiplier
    )
    normalized_probabilities = jnp.exp(scores - logsum[..., None])
    probability_gradient = jnp.einsum(
        "cog,cmg->com", output_gradient, value_rows, preferred_element_type=jnp.float32
    )
    inner_sum = jnp.sum(normalized_probabilities * probability_gradient, -1, keepdims=True)
    score_gradient = (normalized_probabilities * (probability_gradient - inner_sum)).astype(
        jnp.bfloat16
    )
    grad_queries = (
        jnp.einsum(
            "eap,epj->eaj", score_gradient, key_tile_block, preferred_element_type=jnp.float32
        )
        * scaling_multiplier
    )
    grad_keys = (
        jnp.einsum(
            "rsa,rsj->raj", score_gradient, query_rows_all, preferred_element_type=jnp.float32
        )
        * scaling_multiplier
    )
    grad_values = jnp.einsum(
        "rsa,rsj->raj",
        normalized_probabilities.astype(jnp.bfloat16),
        output_gradient,
        preferred_element_type=jnp.float32,
    )
    return jnp.concatenate([grad_queries, grad_keys, grad_values], -1).astype(jnp.bfloat16)


def per_device(latents, cond, cotangent, w_qkv, w_out, w_up, w_down, w_ada, b_ada):
    batch_dev, tokens_dev, model_width = latents.shape
    row_count = batch_dev * tokens_dev
    cond_wide = cond.astype(jnp.float32)
    cond_act, silu_back = jax.vjp(jax.nn.silu, cond_wide)
    cond_all = lax.all_gather(cond_act.astype(jnp.bfloat16), "fsdp", axis=0, tiled=True)
    mod_cols = (
        jnp.dot(cond_all, w_ada, preferred_element_type=jnp.float32) + b_ada.astype(jnp.float32)
    ).astype(jnp.bfloat16)
    modulation = lax.all_to_all(mod_cols, "fsdp", split_axis=0, concat_axis=1, tiled=True).astype(
        jnp.float32
    )
    shift_one, scale_one, gate_one, shift_two, scale_two, gate_two = [
        modulation[:, None, position * model_width : (position + 1) * model_width]
        for position in range(6)
    ]
    qkv_full, out_full, up_full, down_full = (
        lax.all_gather(w_qkv, "fsdp", axis=0, tiled=True),
        lax.all_gather(w_out, "fsdp", axis=0, tiled=True),
        lax.all_gather(w_up, "fsdp", axis=0, tiled=True),
        lax.all_gather(w_down, "fsdp", axis=1, tiled=True),
    )
    inputs = latents.astype(jnp.float32)
    normed_one, inverse_one = normalize(inputs)
    hidden_one = (
        (normed_one * (1.0 + scale_one) + shift_one)
        .astype(jnp.bfloat16)
        .reshape(row_count, model_width)
    )
    qkv_rows = jnp.dot(hidden_one, qkv_full, preferred_element_type=jnp.float32).astype(
        jnp.bfloat16
    )
    qkv_tokens = qkv_rows.reshape(batch_dev, tokens_dev, H, 3 * HD)
    qkv_heads = jnp.moveaxis(
        lax.all_to_all(qkv_tokens, "seq", split_axis=2, concat_axis=1, tiled=True), 2, 0
    )
    attention_result, logsum = lax.map(head_forward, qkv_heads)
    attn_tokens = lax.all_to_all(
        jnp.moveaxis(attention_result, 0, 2), "seq", split_axis=1, concat_axis=2, tiled=True
    )
    attn_rows = attn_tokens.reshape(row_count, model_width)
    branch_one = jnp.dot(attn_rows, out_full, preferred_element_type=jnp.float32).reshape(
        batch_dev, tokens_dev, model_width
    )
    middle = inputs + gate_one * branch_one
    normed_two, inverse_two = normalize(middle)
    hidden_two = (normed_two * (1.0 + scale_two) + shift_two).astype(jnp.bfloat16)
    grad_mixed = cotangent.astype(jnp.float32)
    grad_branch_two = (gate_two * grad_mixed).astype(jnp.bfloat16)
    hidden_all, grad_all = (
        lax.all_gather(hidden_two, "seq", axis=1, tiled=True),
        lax.all_gather(grad_branch_two, "seq", axis=1, tiled=True),
    )
    full_rows = batch_dev * hidden_all.shape[1]
    hidden_rows = hidden_all.reshape(full_rows, model_width)
    grad_rows = grad_all.reshape(full_rows, model_width)
    up_values = jnp.dot(hidden_rows, up_full, preferred_element_type=jnp.float32)
    activated, gelu_back = jax.vjp(partial(jax.nn.gelu, approximate=True), up_values)
    activated_low = activated.astype(jnp.bfloat16)
    branch_part = jnp.dot(activated_low, down_full, preferred_element_type=jnp.float32)
    grad_act = jnp.dot(grad_rows, down_full.T, preferred_element_type=jnp.float32)
    grad_up_values = gelu_back(grad_act)[0].astype(jnp.bfloat16)
    term_down = jnp.dot(activated_low.T, grad_rows, preferred_element_type=jnp.float32)
    term_up = jnp.dot(hidden_rows.T, grad_up_values, preferred_element_type=jnp.float32)
    grad_part = jnp.dot(grad_up_values, up_full.T, preferred_element_type=jnp.float32)
    branch_two, grad_hidden_two = (
        lax.psum_scatter(
            branch_part.reshape(batch_dev, -1, model_width).astype(jnp.bfloat16),
            "seq",
            scatter_dimension=1,
            tiled=True,
        ).astype(jnp.float32),
        lax.psum_scatter(
            grad_part.reshape(batch_dev, -1, model_width).astype(jnp.bfloat16),
            "seq",
            scatter_dimension=1,
            tiled=True,
        ).astype(jnp.float32),
    )
    mixed = (middle + gate_two * branch_two).astype(jnp.bfloat16)
    grad_gate_two = jnp.sum(grad_mixed * branch_two, 1)
    grad_shift_two = jnp.sum(grad_hidden_two, 1)
    grad_scale_two = jnp.sum(grad_hidden_two * normed_two, 1)
    grad_middle = grad_mixed + norm_grad(
        normed_two, inverse_two, grad_hidden_two * (1.0 + scale_two)
    )
    grad_gate_one = jnp.sum(grad_middle * branch_one, 1)
    grad_branch_one = (gate_one * grad_middle).astype(jnp.bfloat16).reshape(row_count, model_width)
    term_out = jnp.dot(attn_rows.T, grad_branch_one, preferred_element_type=jnp.float32)
    grad_attn = (
        jnp.dot(grad_branch_one, out_full.T, preferred_element_type=jnp.float32)
        .astype(jnp.bfloat16)
        .reshape(batch_dev, tokens_dev, H, HD)
    )
    grad_attn_heads = jnp.moveaxis(
        lax.all_to_all(grad_attn, "seq", split_axis=2, concat_axis=1, tiled=True), 2, 0
    )
    grad_qkv_heads = lax.map(head_backward, (qkv_heads, logsum, grad_attn_heads))
    grad_qkv_rows = lax.all_to_all(
        jnp.moveaxis(grad_qkv_heads, 0, 2), "seq", split_axis=1, concat_axis=2, tiled=True
    ).reshape(row_count, 3 * model_width)
    term_qkv = jnp.dot(hidden_one.T, grad_qkv_rows, preferred_element_type=jnp.float32)
    grad_hidden_one = jnp.dot(
        grad_qkv_rows, qkv_full.T, preferred_element_type=jnp.float32
    ).reshape(batch_dev, tokens_dev, model_width)
    grad_shift_one = jnp.sum(grad_hidden_one, 1)
    grad_scale_one = jnp.sum(grad_hidden_one * normed_one, 1)
    grad_latents = grad_middle + norm_grad(
        normed_one, inverse_one, grad_hidden_one * (1.0 + scale_one)
    )
    grad_mod_part = jnp.concatenate(
        [
            grad_shift_one,
            grad_scale_one,
            grad_gate_one,
            grad_shift_two,
            grad_scale_two,
            grad_gate_two,
        ],
        -1,
    )
    grad_mod = lax.psum(grad_mod_part, "seq").astype(jnp.bfloat16)
    grad_mod_cols = lax.all_to_all(grad_mod, "fsdp", split_axis=1, concat_axis=0, tiled=True)
    grad_w_ada = jnp.dot(cond_all.T, grad_mod_cols, preferred_element_type=jnp.float32)
    grad_b_ada = jnp.sum(grad_mod_cols.astype(jnp.float32), 0)
    cond_term = jnp.dot(grad_mod_cols, w_ada.T, preferred_element_type=jnp.float32)
    sectioned = (
        lax.psum_scatter(
            term_qkv.astype(jnp.bfloat16), "fsdp", scatter_dimension=0, tiled=True
        ).astype(jnp.float32),
        lax.psum_scatter(
            term_out.astype(jnp.bfloat16), "fsdp", scatter_dimension=0, tiled=True
        ).astype(jnp.float32),
        lax.psum_scatter(
            term_up.astype(jnp.bfloat16), "fsdp", scatter_dimension=0, tiled=True
        ).astype(jnp.float32),
        lax.psum_scatter(
            term_down.astype(jnp.bfloat16), "fsdp", scatter_dimension=1, tiled=True
        ).astype(jnp.float32),
        lax.psum_scatter(
            cond_term.astype(jnp.bfloat16), "fsdp", scatter_dimension=0, tiled=True
        ).astype(jnp.float32),
    )
    grad_w_qkv, grad_w_out = (
        lax.psum(sectioned[0].astype(jnp.bfloat16), "seq").astype(jnp.float32),
        lax.psum(sectioned[1].astype(jnp.bfloat16), "seq").astype(jnp.float32),
    )
    grad_w_up = sectioned[2]
    grad_w_down = sectioned[3]
    cond_sum = sectioned[4]
    grad_cond = silu_back(cond_sum)[0]
    return (
        mixed,
        grad_latents,
        grad_cond,
        grad_w_qkv,
        grad_w_out,
        grad_w_up,
        grad_w_down,
        grad_w_ada,
        grad_b_ada,
    )


def solution(mesh):
    return jax.shard_map(
        per_device,
        mesh=mesh,
        in_specs=(
            P("fsdp", "seq", None),
            P("fsdp", None),
            P("fsdp", "seq", None),
            P("fsdp", None),
            P("fsdp", None),
            P("fsdp", "seq"),
            P("seq", "fsdp"),
            P(None, "fsdp"),
            P("fsdp"),
        ),
        out_specs=(
            P("fsdp", "seq", None),
            P("fsdp", "seq", None),
            P("fsdp", None),
            P("fsdp", None),
            P("fsdp", None),
            P("fsdp", "seq"),
            P("seq", "fsdp"),
            P(None, "fsdp"),
            P("fsdp"),
        ),
        check_vma=False,
    )
```

profile of v0, /device:TPU:0, one launch (start us, length us, event | category | flops | bytes accessed | tf_op | source)
XLA Modules:
  0.0 784.8 jit_solution(12283877968619455743)
XLA Ops:
  10.7 23.4 %all-gather = bf16[16,1,1024]{2,1,0:T(2,128)(2,1)S(1)} all-gather(bf16[1,1,1024]{2,1,0:T(2,128)(2,1)S(1)} %get-tuple-element.94), channel_id=1, replica_groups=mesh['fsdp'=16,'seq'=2] {'fsdp'}, dimensions={0}, use_global_device_ids=true | all-gather | bytes 34816 | tf_op jit(solution)/shard_map/all_gather | solution.py:97
  47.0 28.2 %all-gather.8.cloned.1.call-done = bf16[1024,3072]{1,0:T(8,128)(2,1)} async-done(((bf16[64,3072]{1,0:T(8,128)(2,1)}), bf16[1024,3072]{1,0:T(8,128)(2,1)}) %all-gather.8.cloned.1.call-update) | async-done | bytes 6291472 | tf_op jit(solution)/shard_map/all_gather | solution.py:109
  75.1 7.8 convolution_convert_fusion.1
  93.6 36.0 %all-to-all-done.1 = bf16[1,512,16,192]{1,3,0,2:T(8,128)(2,1)} async-done(((bf16[1,512,16,192]{1,3,0,2:T(8,128)(2,1)}), bf16[1,512,16,192]{1,3,0,2:T(8,128)(2,1)}, u32[]{:S(2)}, u32[]{:S(2)}) %all-to-all-start.1) | async-done | bytes 3145760 | tf_op jit(solution)/shard_map/all_to_all | solution.py:126
  135.9 28.9 %while.22 = (s32[]{:T(128)}, bf16[8,1,1024,64]{2,3,1,0:T(8,128)(2,1)S(1)}, f32[8,1,1024]{2,1,0:T(1,128)S(1)}, bf16[8,1,1024,192]{3,2,1,0:T(8,128)(2,1)}, s32[]{:T(128)}) while((s32[]{:T(128)}, bf16[8,1,1024,64]{2,3,1,0:T(8,128)(2,1)S(1)}, f32[8,1,1024]{2,1,0:T(1,128)S(1)}, bf16[8,1,1024,192]{3,2,1,0:T(8,128)(2,1)}, s32[]{:T(128)}) %tuple.93), condition=%wide.region_5.6_spmd, body=%wide.region_2.5_spmd.sunk | while | flops 277937152 | bytes 14196809 | solution.py:128
  172.7 16.7 %all_to_all.95 = bf16[2,2,131072]{2,1,0:T(2,128)(2,1)} all-to-all(bf16[2,2,131072]{2,1,0:T(2,128)(2,1)S(1)} %reshape.383), channel_id=1, replica_groups=mesh['fsdp'=16,'seq'=2] {'seq'}, dimensions={0} | all-to-all | bytes 2097152 | tf_op jit(solution)/shard_map/all_to_all | solution.py:129
  207.1 27.3 %all-gather.12.cloned.1.call-done = bf16[1,1024,1024]{2,1,0:T(8,128)(2,1)} async-done(((bf16[1,512,1024]{2,1,0:T(8,128)(2,1)}), bf16[1,1024,1024]{2,1,0:T(8,128)(2,1)}) %all-gather.12.cloned.1.call-update) | async-done | bytes 2097168 | tf_op jit(solution)/shard_map/all_gather | solution.py:142
  234.4 10.9 %fusion.68 = f32[1024,2048]{1,0:T(8,128)} fusion(bf16[1024,2048]{1,0:T(8,128)(2,1)} %all-gather.14.cloned.1.call-done, bf16[1,1024,1024]{2,1,0:T(8,128)(2,1)} %all-gather.12.cloned.1.call-done), kind=kOutput, calls=%fused_computation.99 | convolution fusion | flops 4294967296 | bytes 14680064 | tf_op jit(solution)/shard_map/dot_general | solution.py:148
  245.3 23.7 %all-gather.18.cloned.1.call-done = bf16[1,1024,1024]{2,1,0:T(8,128)(2,1)} async-done(((bf16[1,512,1024]{2,1,0:T(8,128)(2,1)}), bf16[1,1024,1024]{2,1,0:T(8,128)(2,1)}) %all-gather.18.cloned.1.call-update) | async-done | bytes 2097168 | tf_op jit(solution)/shard_map/all_gather | solution.py:143
  268.9 52.8 %all-gather.16.cloned.1.call-done = bf16[2048,1024]{0,1:T(8,128)(2,1)} async-done(((bf16[2048,64]{0,1:T(8,128)(2,1)}), bf16[2048,1024]{0,1:T(8,128)(2,1)}) %all-gather.16.cloned.1.call-update) | async-done | bytes 4194320 | tf_op jit(solution)/shard_map/all_gather | solution.py:112
  321.7 12.5 %fusion.35 = bf16[1024,2048]{1,0:T(8,128)(2,1)S(1)} fusion(f32[1024,2048]{1,0:T(8,128)} %fusion.68, bf16[2048,1024]{0,1:T(8,128)(2,1)} %all-gather.16.cloned.1.call-done, bf16[1,1024,1024]{2,1,0:T(8,128)(2,1)} %all-gather.18.cloned.1.call-done), kind=kOutput, calls=%fused_computation.52 | convolution fusion | flops 4336910336 | bytes 18874368 | tf_op jit(solution)/shard_map/dot_general | solution.py:152
  342.3 11.2 %convert_bitcast_fusion.1 = bf16[1,1024,1024]{2,1,0:T(8,128)(2,1)} fusion(bf16[2048,1024]{0,1:T(8,128)(2,1)} %all-gather.16.cloned.1.call-done, f32[1024,2048]{1,0:T(8,128)} %fusion.68), kind=kOutput, calls=%fused_computation.103 | convolution fusion | flops 4314890240 | bytes 14680064 | tf_op jit(solution)/shard_map/dot_general | solution.py:151
  353.6 9.5 %convolution_convert_fusion.3 = bf16[1024,2048]{1,0:T(8,128)(2,1)} fusion(bf16[1024,2048]{1,0:T(8,128)(2,1)} %copy-done.23, bf16[1,1024,1024]{2,1,0:T(8,128)(2,1)} %all-gather.12.cloned.1.call-done), kind=kOutput, calls=%fused_computation.57 | convolution fusion | flops 4297064448 | bytes 10485760 | tf_op jit(solution)/shard_map/dot_general | solution.py:155
  363.3 10.8 %convolution_convert_fusion.2 = bf16[2048,1024]{0,1:T(8,128)(2,1)} fusion(bf16[1,1024,1024]{2,1,0:T(8,128)(2,1)} %all-gather.18.cloned.1.call-done, f32[1024,2048]{1,0:T(8,128)} %fusion.68), kind=kOutput, calls=%fused_computation.56 | convolution fusion | flops 4315938816 | bytes 14680064 | tf_op jit(solution)/shard_map/dot_general | solution.py:154
  376.3 30.4 %reduce-scatter.7.cloned.1.call-done = bf16[1,512,1024]{2,1,0:T(8,128)(2,1)} async-done(((bf16[1,1024,1024]{2,1,0:T(8,128)(2,1)}), bf16[1,512,1024]{2,1,0:T(8,128)(2,1)}) %reduce-scatter.7.cloned.1.call-update) | async-done | bytes 1048592 | tf_op jit(solution)/shard_map/reduce_scatter | solution.py:158
  425.6 9.7 %all-to-all-done.3 = bf16[1,512,16,64]{1,3,0,2:T(8,128)(2,1)} async-done(((bf16[1,512,16,64]{1,3,0,2:T(8,128)(2,1)}), bf16[1,512,16,64]{1,3,0,2:T(8,128)(2,1)}, u32[]{:S(2)}, u32[]{:S(2)}) %all-to-all-start.3) | async-done | bytes 1048608 | tf_op jit(solution)/shard_map/all_to_all | solution.py:187
  437.4 56.1 %while.23 = (s32[]{:T(128)}, bf16[8,1,1024,192]{2,3,1,0:T(8,128)(2,1)}, bf16[8,1,1024,192]{3,2,1,0:T(8,128)(2,1)}, f32[8,1,1024]{2,1,0:T(1,128)S(1)}, bf16[8,1,1024,64]{3,2,1,0:T(8,128)(2,1)S(1)}, /*index=5*/s32[]{:T(128)}) while((s32[]{:T(128)}, bf16[8,1,1024,192]{2,3,1,0:T(8,128)(2,1)}, bf16[8,1,1024,192]{3,2,1,0:T(8,128)(2,1)}, ...), condition=%wide.region_14.15_spmd, body=%wide.region_12.14_spmd.sunk | while | flops 685177856 | bytes 35156564 | solution.py:189
  500.5 54.2 %all_to_all.96 = bf16[1,1024,8,192]{3,2,0,1:T(8,128)(2,1)} all-to-all(bf16[1,1024,8,192]{3,2,0,1:T(8,128)(2,1)} %bitcast.208), channel_id=1, replica_groups=mesh['fsdp'=16,'seq'=2] {'seq'}, dimensions={1} | all-to-all | bytes 6291456 | tf_op jit(solution)/shard_map/all_to_all | solution.py:190
  554.7 8.2 %copy.70 = bf16[1,2,512,8,192]{2,1,4,3,0:T(2,128)(2,1)} copy(bf16[1,2,512,8,192]{4,3,2,1,0:T(8,128)(2,1)} %bitcast.209) | data formatting | bytes 6291456 | tf_op jit(solution)/shard_map/all_to_all | solution.py:190
  578.0 7.2 fusion.51
  586.9 9.8 %psum.21 = bf16[1,6144]{1,0:T(2,128)(2,1)S(1)} all-reduce(f32[1,6144]{1,0:T(1,128)S(1)} %constant_dynamic-update-slice_fusion.1), channel_id=1, replica_groups=mesh['fsdp'=16,'seq'=2] {'seq'}, use_global_device_ids=true, to_apply=%region_23.24 | all-reduce | flops 6144 | bytes 36864 | tf_op jit(solution)/shard_map/psum | solution.py:213
  610.6 12.6 %reduce-scatter.13.cloned.1.call-done = bf16[64,1024]{1,0:T(8,128)(2,1)} async-done(((bf16[1024,1024]{1,0:T(8,128)(2,1)}), bf16[64,1024]{1,0:T(8,128)(2,1)}) %reduce-scatter.13.cloned.1.call-update) | async-done | bytes 131088 | tf_op jit(solution)/shard_map/reduce_scatter | solution.py:222
  623.2 88.5 %reduce-scatter.11.cloned.1.call-done = bf16[64,3072]{1,0:T(8,128)(2,1)} async-done(((bf16[1024,3072]{1,0:T(8,128)(2,1)}), bf16[64,3072]{1,0:T(8,128)(2,1)}) %reduce-scatter.11.cloned.1.call-update) | async-done | bytes 393232 | tf_op jit(solution)/shard_map/reduce_scatter | solution.py:219
  712.3 59.1 %all-reduce = bf16[16,1024]{1,0:T(8,128)(2,1)S(1)} all-reduce(bf16[16,1024]{1,0:T(8,128)(2,1)S(1)} %convolution_convert_fusion.6), channel_id=4, replica_groups=mesh['fsdp'=16,'seq'=2] {'fsdp'}, use_global_device_ids=true, to_apply=%region_24.25.clone | all-reduce | flops 16384 | bytes 65536
  (270 shorter events, 219.1 us)
Async XLA Ops:
  7.2 67.9 %all-gather.8.cloned.1.call-start = ((), (), s32[]{:S(2)}) async-start(), calls=%async_computation.12 | async-start | bytes 6684672 | tf_op jit(solution)/shard_map/all_gather | solution.py:109
  7.9 189.0 %all-gather.10.cloned.1.call-start = ((), (), s32[]{:S(2)}) async-start(), calls=%async_computation.13 | async-start | bytes 2228224 | tf_op jit(solution)/shard_map/all_gather | solution.py:110
  36.7 10.0 %all-to-all-start = ((bf16[16,2,192]{2,1,0:T(2,128)(2,1)}), bf16[16,2,192]{2,1,0:T(2,128)(2,1)S(1)}, u32[]{:S(2)}, u32[]{:S(2)}) async-start(bf16[16,2,192]{2,1,0:T(2,128)(2,1)} %reshape.381), calls=%async_computation | async-start | bytes 32768 | tf_op jit(solution)/shard_map/all_to_all | solution.py:101
  41.7 41.2 %copy-start.13 = (f32[512]{0:T(512)}, f32[512]{0:T(512)S(1)}, u32[]{:S(2)}) copy-start(f32[512]{0:T(512)S(1)} %broadcast_multiply_fusion.5) | copy-start | bytes 6148
  42.1 40.8 %copy-start.17 = (f32[512]{0:T(512)}, f32[512]{0:T(512)S(1)}, u32[]{:S(2)}) copy-start(f32[512]{0:T(512)S(1)} %add_rsqrt_fusion.1) | copy-start | bytes 6148
  46.9 36.0 %copy-start.11 = (f32[1,1024]{1,0:T(1,128)}, f32[1,1024]{1,0:T(1,128)S(1)}, u32[]{:S(2)}) copy-start(f32[1,1024]{1,0:T(1,128)S(1)} %get-tuple-element.107) | copy-start | bytes 12292
  46.9 36.0 %copy-start.19 = (f32[1,1024]{1,0:T(1,128)}, f32[1,1024]{1,0:T(1,128)S(1)}, u32[]{:S(2)}) copy-start(f32[1,1024]{1,0:T(1,128)S(1)} %get-tuple-element.105) | copy-start | bytes 12292
  87.6 42.1 %all-to-all-start.1 = ((bf16[1,512,16,192]{1,3,0,2:T(8,128)(2,1)}), bf16[1,512,16,192]{1,3,0,2:T(8,128)(2,1)}, u32[]{:S(2)}, u32[]{:S(2)}) async-start(bf16[1,512,16,192]{1,3,0,2:T(8,128)(2,1)} %bitcast.211), calls=%async_computation.1 | async-start | bytes 6291456 | tf_op jit(solution)/shard_map/all_to_all | solution.py:126
  92.8 114.3 %all-gather.14.cloned.1.call-start = ((), (), s32[]{:S(2)}) async-start(), calls=%async_computation.15 | async-start | bytes 4456448 | tf_op jit(solution)/shard_map/all_gather | solution.py:111
  93.6 140.8 %all-gather.12.cloned.1.call-start = ((), (), s32[]{:S(2)}) async-start(), calls=%async_computation.14 | async-start | bytes 3145728 | tf_op jit(solution)/shard_map/all_gather | solution.py:142
  203.5 65.5 %all-gather.18.cloned.1.call-start = ((), (), s32[]{:S(2)}) async-start(), calls=%async_computation.18 | async-start | bytes 3145728 | tf_op jit(solution)/shard_map/all_gather | solution.py:143
  206.0 115.7 %all-gather.16.cloned.1.call-start = ((), (), s32[]{:S(2)}) async-start(), calls=%async_computation.16 | async-start | bytes 4456448 | tf_op jit(solution)/shard_map/all_gather | solution.py:112
  206.6 167.6 %reduce-scatter.9.cloned.1.call-start = ((), (), s32[]{:S(2)}) async-start(), calls=%async_computation.19 | async-start | bytes 3145728 | tf_op jit(solution)/shard_map/reduce_scatter | solution.py:164
  342.1 64.7 %reduce-scatter.7.cloned.1.call-start = ((), (), s32[]{:S(2)}) async-start(), calls=%async_computation.17 | async-start | bytes 3145728 | tf_op jit(solution)/shard_map/reduce_scatter | solution.py:158
  353.5 220.9 %reduce-scatter.15.cloned.1.call-start = ((), (), s32[]{:S(2)}) async-start(), calls=%async_computation.22 | async-start | bytes 4456448 | tf_op jit(solution)/shard_map/reduce_scatter | solution.py:225
  363.1 213.1 %reduce-scatter.17.cloned.1.call-start = ((), (), s32[]{:S(2)}) async-start(), calls=%async_computation.23 | async-start | bytes 4456448 | tf_op jit(solution)/shard_map/reduce_scatter | solution.py:228
  416.9 18.4 %all-to-all-start.3 = ((bf16[1,512,16,64]{1,3,0,2:T(8,128)(2,1)}), bf16[1,512,16,64]{1,3,0,2:T(8,128)(2,1)}, u32[]{:S(2)}, u32[]{:S(2)}) async-start(bf16[1,512,16,64]{1,3,0,2:T(8,128)(2,1)} %bitcast.215), calls=%async_computation.5 | async-start | bytes 2097152 | tf_op jit(solution)/shard_map/all_to_all | solution.py:187
  421.4 201.8 %reduce-scatter.13.cloned.1.call-start = ((), (), s32[]{:S(2)}) async-start(), calls=%async_computation.21 | async-start | bytes 2228224 | tf_op jit(solution)/shard_map/reduce_scatter | solution.py:222
  425.3 286.4 %reduce-scatter.11.cloned.1.call-start = ((), (), s32[]{:S(2)}) async-start(), calls=%async_computation.20 | async-start | bytes 6684672 | tf_op jit(solution)/shard_map/reduce_scatter | solution.py:219
  598.0 12.2 %all-to-all-start.5 = ((bf16[16,2,192]{2,1,0:T(2,128)(2,1)}), bf16[16,2,192]{2,1,0:T(2,128)(2,1)S(1)}, u32[]{:S(2)}, u32[]{:S(2)}) async-start(bf16[16,2,192]{2,1,0:T(2,128)(2,1)} %reshape.385), calls=%async_computation.7 | async-start | bytes 32768 | tf_op jit(solution)/shard_map/all_to_all | solution.py:214
  603.7 170.6 %all-reduce.4.cloned.1.call-start = ((), (), s32[]{:S(2)}) async-start(), calls=%async_computation.24 | async-start | bytes 1048576 | tf_op jit(solution)/shard_map/psum | solution.py:236
  603.8 167.7 %copy-start.15 = (bf16[1,1024]{1,0:T(2,128)(2,1)S(1)}, bf16[1,1024]{1,0:T(2,128)(2,1)}, u32[]{:S(2)}) copy-start(bf16[1,1024]{1,0:T(2,128)(2,1)} %param.14) | copy-start | bytes 6148
  603.8 167.7 %copy-start.16 = (f32[1,1024]{1,0:T(1,128)S(1)}, f32[1,1024]{1,0:T(1,128)}, u32[]{:S(2)}) copy-start(f32[1,1024]{1,0:T(1,128)} %get-tuple-element.95) | copy-start | bytes 12292
  603.8 168.9 %copy-start.10 = (bf16[16,1,1024]{2,1,0:T(2,128)(2,1)S(1)}, bf16[16,1,1024]{2,1,0:T(2,128)(2,1)}, u32[]{:S(2)}) copy-start(bf16[16,1,1024]{2,1,0:T(2,128)(2,1)} %copy-done.9) | copy-start | bytes 98308
  (17 other events, 118.9 us)
Sparse Core Ops, SparseCore 0:
  10.3 64.7 all-gather.7
  77.3 39.9 all-gather.9
  119.5 49.5 all-gather.13
  203.6 30.7 all-gather.11
  235.8 33.1 all-gather.17
  271.0 50.7 all-gather.15
  342.2 30.3 reduce-scatter.8
  374.9 31.8 reduce-scatter.6
  410.6 72.4 reduce-scatter.14
  487.3 71.3 reduce-scatter.16
  562.5 60.6 reduce-scatter.12
  627.5 84.1 reduce-scatter.10
  714.0 27.9 all-reduce.3
where the time goes:
time: 795 us; the launch traced here: 785 us
  waiting for transfers between devices  319 us (40%)
  blocking collectives  163 us (21%)
  matrix products  140 us (18%)
  local copies, waits for them, and re-layouts  76.5 us (10%)
  other arithmetic  50.7 us (6%)
  starting transfers between devices  20.4 us (3%)
  between operations  14.8 us (2%)
    reduce_scatter x1, waiting for transfers between devices, per_device(): lax.psum_scatter(term_qkv.astype(jnp.bfloat16), 'fsdp', scatter_dimension...  88.5 us
    unnamed x1, blocking collectives  59.1 us
    all_to_all x1, blocking collectives, per_device(): lax.all_to_all(jnp.moveaxis(grad_qkv_heads, 0, 2), 'seq', split_axis=1, c...  54.2 us
    all_gather x1, waiting for transfers between devices, per_device(): lax.all_gather(w_down, 'fsdp', axis=1, tiled=True)  52.8 us
    all_to_all x1, waiting for transfers between devices, per_device(): lax.all_to_all(qkv_tokens, 'seq', split_axis=2, concat_axis=1, tiled=True)  36 us
    reduce_scatter x1, waiting for transfers between devices, per_device(): lax.psum_scatter(branch_part.reshape(batch_dev, -1, model_width).astype(j...  30.4 us
    all_gather x1, waiting for transfers between devices, per_device(): lax.all_gather(w_qkv, 'fsdp', axis=0, tiled=True)  28.2 us
    all_gather x1, waiting for transfers between devices, per_device(): lax.all_gather(hidden_two, 'seq', axis=1, tiled=True)  27.3 us
  transfers between devices with their start and end apart: 17, of which 11 were waited for; matrix products, arithmetic and copies ran while one was open for 30% of the time, Pallas kernels for 0%

commit v1 on v0

v1 whole, which is shorter than its diff:
```python
from functools import partial

import jax
import jax.numpy as jnp
from jax import lax
from jax.experimental import pallas as pl
from jax.experimental.pallas import tpu as pltpu
from jax.sharding import PartitionSpec as P

H = 16
HD = 64
EPSILON = 1e-06
LOG2E = 1.4426950408889634
SCALE2 = HD**-0.5 * LOG2E
VMEM = 56 * 1024 * 1024
CHUNK = 256

NT = (((1,), (1,)), ((), ()))
TN = (((0,), (0,)), ((), ()))
NN = (((1,), (0,)), ((), ()))


def mm(a, b, dims=NN):
    return lax.dot_general(a, b, dims, preferred_element_type=jnp.float32)


def normalize(value_rows):
    center = value_rows - jnp.mean(value_rows, -1, keepdims=True)
    inverse = lax.rsqrt(jnp.mean(center * center, -1, keepdims=True) + EPSILON)
    return (center * inverse, inverse)


def norm_grad(normed, inverse, grad_normed):
    return inverse * (
        grad_normed
        - jnp.mean(grad_normed, -1, keepdims=True)
        - normed * jnp.mean(grad_normed * normed, -1, keepdims=True)
    )


def head_parts(ref, head, rows=slice(None)):
    base = head * 3 * HD
    return [ref[rows, base + j * HD : base + (j + 1) * HD] for j in range(3)]


def attend_kernel(query_ref, all_ref, out_ref, lse_ref):
    rows = query_ref.shape[0]
    for head in range(2):
        _, keys, values = head_parts(all_ref, head)
        chunk = min(CHUNK, rows)
        for at in range(0, rows, chunk):
            span = slice(at, at + chunk)
            queries = head_parts(query_ref, head, span)[0]
            scores = mm(keys, queries, NT)
            highest = jnp.max(scores, 0, keepdims=True)
            raised = jnp.exp2(scores * SCALE2 - highest * SCALE2)
            totals = jnp.sum(raised, 0, keepdims=True)
            result = mm(values, raised.astype(jnp.bfloat16), TN) / totals
            out_ref[span, head * HD : (head + 1) * HD] = result.T.astype(jnp.bfloat16)
            lse_ref[0, head : head + 1, span] = highest * SCALE2 + jnp.log2(totals)


def attend(qkv, tokens, first, count):
    length, columns = qkv.shape
    pairs = columns // (6 * HD)
    return pl.pallas_call(
        attend_kernel,
        grid=(pairs, count),
        in_specs=[
            pl.BlockSpec((tokens, 6 * HD), lambda p, b: (first + b, p)),
            pl.BlockSpec((length, 6 * HD), lambda p, b: (0, p)),
        ],
        out_specs=[
            pl.BlockSpec((tokens, 2 * HD), lambda p, b: (b, p)),
            pl.BlockSpec((1, 2, tokens), lambda p, b: (p, 0, b)),
        ],
        out_shape=[
            jax.ShapeDtypeStruct((count * tokens, pairs * 2 * HD), jnp.bfloat16),
            jax.ShapeDtypeStruct((pairs, 2, count * tokens), jnp.float32),
        ],
        compiler_params=pltpu.CompilerParams(vmem_limit_bytes=VMEM),
        cost_estimate=pl.CostEstimate(
            flops=4 * pairs * 2 * HD * length * count * tokens * 4,
            bytes_accessed=2 * length * columns,
            transcendentals=pairs * 2 * length * count * tokens,
        ),
        name="attend",
    )(qkv, qkv)


def attend_back_kernel(all_ref, grad_ref, lse_ref, delta_ref, out_ref, key_acc, value_acc):
    length = all_ref.shape[0]
    scaling = HD**-0.5
    for head in range(2):
        base = head * 3 * HD
        _, keys, values = head_parts(all_ref, head)
        for at in range(0, length, CHUNK):
            span = slice(at, at + CHUNK)
            queries = head_parts(all_ref, head, span)[0]
            grads = grad_ref[span, head * HD : (head + 1) * HD]
            lse = lse_ref[0, head : head + 1, span]
            delta = delta_ref[0, head : head + 1, span]
            probs = jnp.exp2(mm(keys, queries, NT) * SCALE2 - lse)
            score_grad = (probs * (mm(values, grads, NT) - delta)).astype(jnp.bfloat16)
            value_part = mm(probs.astype(jnp.bfloat16), grads)
            key_part = mm(score_grad, queries)
            if at == 0:
                value_acc[...] = value_part
                key_acc[...] = key_part
            else:
                value_acc[...] += value_part
                key_acc[...] += key_part
            query_grad = mm(keys, score_grad, TN) * scaling
            out_ref[span, base : base + HD] = query_grad.T.astype(jnp.bfloat16)
        out_ref[:, base + HD : base + 2 * HD] = (key_acc[...] * scaling).astype(jnp.bfloat16)
        out_ref[:, base + 2 * HD : base + 3 * HD] = value_acc[...].astype(jnp.bfloat16)


def attend_back(qkv, grad_attn, lse, delta):
    length, columns = qkv.shape
    pairs = columns // (6 * HD)
    return pl.pallas_call(
        attend_back_kernel,
        grid=(pairs,),
        in_specs=[
            pl.BlockSpec((length, 6 * HD), lambda p: (0, p)),
            pl.BlockSpec((length, 2 * HD), lambda p: (0, p)),
            pl.BlockSpec((1, 2, length), lambda p: (p, 0, 0)),
            pl.BlockSpec((1, 2, length), lambda p: (p, 0, 0)),
        ],
        out_specs=pl.BlockSpec((length, 6 * HD), lambda p: (0, p)),
        out_shape=jax.ShapeDtypeStruct((length, columns), jnp.bfloat16),
        scratch_shapes=[
            pltpu.VMEM((length, HD), jnp.float32),
            pltpu.VMEM((length, HD), jnp.float32),
        ],
        compiler_params=pltpu.CompilerParams(vmem_limit_bytes=VMEM),
        cost_estimate=pl.CostEstimate(
            flops=10 * pairs * 2 * HD * length * length * 4,
            bytes_accessed=4 * length * columns,
            transcendentals=pairs * 2 * length * length,
        ),
        name="attend_back",
    )(qkv, grad_attn, lse, delta)


def per_device(sizes, latents, cond, cotangent, w_qkv, w_out, w_up, w_down, w_ada, b_ada):
    shards, splits = sizes["fsdp"], sizes["seq"]
    me = lax.axis_index("seq")
    tokens, width = latents.shape[1:]
    heads = H // splits
    low = jnp.bfloat16
    wide = jnp.float32

    def fetch(value, step):
        return lax.ppermute(value, "seq", [((i + step) % splits, i) for i in range(splits)])

    def send(value, step):
        return lax.ppermute(value, "seq", [(i, (i + step) % splits) for i in range(splits)])

    def everyone(value):
        return [value] + [fetch(value, step) for step in range(1, splits)]

    def in_order(pieces, axis):
        if splits == 1:
            return pieces[0]
        return jnp.concatenate(
            [
                lax.select_n(
                    (position - me) % splits == 1, *pieces
                ) if splits == 2 else
                lax.dynamic_index_in_dim(
                    jnp.stack(pieces), (position - me) % splits, 0, keepdims=False
                )
                for position in range(splits)
            ],
            axis,
        )

    def seq_sum(value):
        if splits != 2:
            return lax.psum(value, "seq").astype(wide)
        return value.astype(wide) + fetch(value, 1).astype(wide)

    spot = lax.axis_index("fsdp")
    depth = shards // 4
    core_at, x_at, z_at = spot % 2, (spot // 2) % 2, spot // 4

    def core_swap(value):
        return lax.ppermute(value, "fsdp", [(i, i ^ 1) for i in range(shards)])

    def x_swap(value):
        return lax.ppermute(value, "fsdp", [(i, i ^ 2) for i in range(shards)])

    def z_send(value, step):
        return lax.ppermute(value, "fsdp", [(i, (i + 4 * step) % shards) for i in range(shards)])

    def two(mine, other, at):
        return jnp.stack(
            [jnp.where(at == 0, mine, other), jnp.where(at == 0, other, mine)], 1
        )

    def gather_rows(shard):
        rows, cols = shard.shape
        line = jnp.zeros((depth, rows, cols), shard.dtype)
        for step in range(depth):
            piece = z_send(shard, step) if step else shard
            line = lax.dynamic_update_slice_in_dim(
                line, piece[None], (z_at - step) % depth, 0
            )
        plane = two(line, x_swap(line), x_at).reshape(2 * depth, rows, cols)
        return two(plane, core_swap(plane), core_at).reshape(shards * rows, cols)

    def halve(value, at, swap):
        mine = lax.dynamic_index_in_dim(value, at, 1, keepdims=False)
        other = lax.dynamic_index_in_dim(value, 1 - at, 1, keepdims=False)
        return (mine.astype(wide) + swap(other).astype(wide)).astype(low)

    def scatter_rows(value):
        rows, cols = value.shape[0] // shards, value.shape[1]
        value = halve(value.reshape(2 * depth, 2, rows, cols), core_at, core_swap)
        value = halve(value.reshape(depth, 2, rows, cols), x_at, x_swap)
        total = lax.dynamic_index_in_dim(value, z_at, 0, keepdims=False).astype(wide)
        for step in range(1, depth):
            piece = lax.dynamic_index_in_dim(value, (z_at + step) % depth, 0, keepdims=False)
            total = total + z_send(piece, step).astype(wide)
        return total

    own_latents, own_cotangent = latents[0], cotangent[0]
    cond_act, silu_back = jax.vjp(jax.nn.silu, cond.astype(wide))
    cond_all = lax.all_to_all(
        jnp.broadcast_to(cond_act.astype(low), (shards, width)),
        "fsdp",
        split_axis=0,
        concat_axis=0,
        tiled=True,
    )
    mod_cols = (mm(cond_all, w_ada) + b_ada.astype(wide)).astype(low)
    modulation = lax.all_to_all(
        mod_cols, "fsdp", split_axis=0, concat_axis=1, tiled=True
    ).astype(wide)
    shift_one, scale_one, gate_one, shift_two, scale_two, gate_two = [
        modulation[:, position * width : (position + 1) * width] for position in range(6)
    ]
    columns = heads * 3 * HD
    qkv_shard = lax.dynamic_slice_in_dim(w_qkv, me * columns, columns, 1)
    qkv_half = lax.all_gather(qkv_shard, "fsdp", axis=0, tiled=True)
    out_full = gather_rows(w_out)
    up_down = lax.all_gather(jnp.concatenate([w_up, w_down.T], 1), "fsdp", axis=0, tiled=True)
    hidden_units = w_up.shape[1]
    up_full, down_full = up_down[:, :hidden_units], up_down[:, hidden_units:]

    latents_all = jnp.concatenate(everyone(own_latents), 0)
    cotangents = everyone(own_cotangent)
    grad_rows = [(gate_two * value.astype(wide)).astype(low) for value in cotangents]

    normed_all, inverse_all = normalize(latents_all.astype(wide))
    hidden_one = (normed_all * (1.0 + scale_one) + shift_one).astype(low)
    qkv = mm(hidden_one, qkv_half).astype(low)
    attn_peers, lse_peers = attend(qkv, tokens, 1, splits - 1)
    peer_rows = [attn_peers[r * tokens : (r + 1) * tokens] for r in range(splits - 1)]
    arrived = [send(value, r + 1) for r, value in enumerate(peer_rows)]
    attn_own, lse_own = attend(qkv, tokens, 0, 1)
    attn_rows = in_order([attn_own] + arrived[::-1], 1)
    branch_one = mm(attn_rows, out_full)
    inputs = own_latents.astype(wide)
    middle = inputs + gate_one * branch_one
    normed_two, inverse_two = normalize(middle)
    hidden_two = (normed_two * (1.0 + scale_two) + shift_two).astype(low)

    hidden_pieces = everyone(hidden_two)
    branch_parts, grad_parts, term_up, term_down = [], [], 0.0, 0.0
    for hidden, grads in zip(hidden_pieces, grad_rows):
        up_values = mm(hidden, up_full)
        activated, gelu_back = jax.vjp(partial(jax.nn.gelu, approximate=True), up_values)
        activated = activated.astype(low)
        grad_up = gelu_back(mm(grads, down_full))[0].astype(low)
        grad_parts.append(mm(grad_up, up_full, NT))
        branch_parts.append(mm(activated, down_full, NT))
        term_up = term_up + mm(hidden, grad_up, TN)
        term_down = term_down + mm(grads, activated, TN)

    def send_parts(parts):
        return [send(parts[step].astype(low), step) for step in range(1, splits)]

    def add_parts(own, received):
        for value in received:
            own = own + value.astype(wide)
        return own

    term_up, term_down = term_up.astype(low), term_down.astype(low)
    grad_sent = send_parts(grad_parts)
    branch_sent = send_parts(branch_parts)
    grad_sent, term_up, term_down = lax.optimization_barrier((grad_sent, term_up, term_down))
    grad_hidden_two = add_parts(grad_parts[0], grad_sent)
    branch_two = add_parts(branch_parts[0], branch_sent)
    grad_w_down = lax.psum_scatter(term_down, "fsdp", scatter_dimension=0, tiled=True)
    grad_w_up = lax.psum_scatter(term_up, "fsdp", scatter_dimension=0, tiled=True)
    grad_mixed = own_cotangent.astype(wide)
    mixed = (middle + gate_two * branch_two).astype(low)
    grad_gate_two = jnp.sum(grad_mixed * branch_two, 0)
    grad_shift_two = jnp.sum(grad_hidden_two, 0)
    grad_scale_two = jnp.sum(grad_hidden_two * normed_two, 0)
    grad_middle = grad_mixed + norm_grad(
        normed_two, inverse_two, grad_hidden_two * (1.0 + scale_two)
    )
    grad_gate_one = jnp.sum(grad_middle * branch_one, 0)
    grad_branch_one = (gate_one * grad_middle).astype(low)

    grad_attn = mm(grad_branch_one, out_full, NT).astype(low)
    own_width = heads * HD
    grad_pieces = [
        lax.dynamic_slice_in_dim(grad_attn, ((me + r) % splits) * own_width, own_width, 1)
        for r in range(splits)
    ]
    grad_arrived = [send(grad_pieces[r], r) for r in range(1, splits)]
    grad_heads = jnp.concatenate([grad_pieces[0]] + grad_arrived[::-1], 0)
    attn_all = jnp.concatenate([attn_own, attn_peers], 0)
    lse = jnp.concatenate([lse_own, lse_peers], 2)
    delta = jnp.sum(
        (grad_heads.astype(wide) * attn_all.astype(wide)).reshape(-1, heads // 2, 2, HD), -1
    ).transpose(1, 2, 0)
    grad_qkv = attend_back(qkv, grad_heads, lse, delta)
    term_out = mm(attn_rows, grad_branch_one, TN)
    grad_w_out = scatter_rows(term_out.astype(low)).astype(low)
    term_qkv = mm(hidden_one, grad_qkv, TN)
    grad_w_qkv = scatter_rows(term_qkv.astype(low)).astype(low)
    hidden_grad_all = mm(grad_qkv, qkv_half, NT)
    grad_shift_one = jnp.sum(hidden_grad_all, 0)
    grad_scale_one = jnp.sum(hidden_grad_all * normed_all, 0)
    hidden_parts = [hidden_grad_all[r * tokens : (r + 1) * tokens] for r in range(splits)]
    grad_hidden_one = add_parts(hidden_parts[0], send_parts(hidden_parts))
    grad_latents = grad_middle + norm_grad(
        normed_all[:tokens], inverse_all[:tokens], grad_hidden_one * (1.0 + scale_one)
    )

    grad_mod = seq_sum(
        jnp.concatenate(
            [
                grad_shift_one,
                grad_scale_one,
                grad_gate_one,
                grad_shift_two,
                grad_scale_two,
                grad_gate_two,
            ]
        )[None]
    ).astype(low)
    grad_mod_cols = lax.all_to_all(grad_mod, "fsdp", split_axis=1, concat_axis=0, tiled=True)
    grad_w_ada = mm(cond_all, grad_mod_cols, TN)
    grad_b_ada = jnp.sum(grad_mod_cols.astype(wide), 0)
    cond_term = mm(grad_mod_cols, w_ada, NT).astype(low)
    cond_terms = lax.all_to_all(cond_term, "fsdp", split_axis=0, concat_axis=0, tiled=True)
    grad_cond = silu_back(jnp.sum(cond_terms.astype(wide), 0, keepdims=True))[0]

    grad_w_qkv = in_order(everyone(grad_w_qkv), 1).astype(wide)
    grad_w_out = seq_sum(grad_w_out)
    return (
        mixed[None],
        grad_latents[None],
        grad_cond,
        grad_w_qkv,
        grad_w_out,
        grad_w_up.astype(wide),
        grad_w_down.T.astype(wide),
        grad_w_ada,
        grad_b_ada,
    )


def solution(mesh):
    return jax.shard_map(
        partial(per_device, dict(mesh.shape)),
        mesh=mesh,
        in_specs=(
            P("fsdp", "seq", None),
            P("fsdp", None),
            P("fsdp", "seq", None),
            P("fsdp", None),
            P("fsdp", None),
            P("fsdp", "seq"),
            P("seq", "fsdp"),
            P(None, "fsdp"),
            P("fsdp"),
        ),
        out_specs=(
            P("fsdp", "seq", None),
            P("fsdp", "seq", None),
            P("fsdp", None),
            P("fsdp", None),
            P("fsdp", None),
            P("fsdp", "seq"),
            P("seq", "fsdp"),
            P(None, "fsdp"),
            P("fsdp"),
        ),
        check_vma=False,
    )
```

time: 795 us -> 407 us (0.51)
  waiting for transfers between devices: 319 us -> 140 us
  blocking collectives: 163 us -> 0 us
  local copies, waits for them, and re-layouts: 76.5 us -> 20.3 us
  Pallas kernels: 0 us -> 55.5 us
  matrix products: 140 us -> 90 us
  starting transfers between devices: 20.4 us -> 46.4 us
  other arithmetic: 50.7 us -> 36 us
    all_gather x6 -> x2, waiting for transfers between devices: 132 us -> 0.01 us  [the longest x1 0.01 us: per_device(): qkv_half = lax.all_gather(qkv_shard, 'fsdp', axis=0, tiled=True)]
    reduce_scatter x6 -> x2, waiting for transfers between devices: 132 us -> 0.01 us  [the longest x1 0.01 us: per_device(): lax.psum_scatter(term_down, 'fsdp', scatter_dimension=0, tiled=True)]
    ppermute x0 -> x26, waiting for transfers between devices: none -> 108 us  [the longest x6 45.3 us: fetch(): lax.ppermute(value, 'seq', [((i + step) % splits, i) for i in range(split...]
    all_to_all x2 -> x0, blocking collectives: 70.9 us -> none  [the longest x1 54.2 us: per_device(): lax.all_to_all(jnp.moveaxis(grad_qkv_heads, 0, 2), 'seq', split_axis=1, c...]
    unnamed x1 -> x0, blocking collectives: 59.1 us -> none
    pallas_call x0 -> x3, Pallas kernels: none -> 55.5 us  [the longest x2 30 us: attend(): pl.pallas_call(attend_kernel, grid=(pairs, count), in_specs=[pl.BlockSpec...]
    dot_general x71 -> x21, matrix products: 140 us -> 90 us  [mm(): return lax.dot_general(a, b, dims, preferred_element_type=jnp.float32)]
    ppermute x0 -> x26, starting transfers between devices: none -> 31.6 us  [the longest x9 15 us: z_send(): lax.ppermute(value, 'fsdp', [(i, (i + 4 * step) % shards) for i in range(...]
  transfers between devices with their start and end apart: 17 -> 34, of which waited for: 11 -> 17; matrix products, arithmetic and copies ran while one was open for 30% -> 32% of each run, Pallas kernels for 0% -> 14%
where the time goes in v1:
time: 407 us; the launch traced here: 403 us
  waiting for transfers between devices  140 us (34%)
  matrix products  90 us (22%)
  Pallas kernels  55.5 us (14%)
  starting transfers between devices  46.4 us (11%)
  other arithmetic  36 us (9%)
  local copies, waits for them, and re-layouts  20.3 us (5%)
  between operations  15 us (4%)
    dot_general x21, matrix products, mm(): return lax.dot_general(a, b, dims, preferred_element_type=jnp.float32)  90 us
    ppermute x6, waiting for transfers between devices, fetch(): lax.ppermute(value, 'seq', [((i + step) % splits, i) for i in range(split...  45.3 us
    pallas_call x2, Pallas kernels, attend(): pl.pallas_call(attend_kernel, grid=(pairs, count), in_specs=[pl.BlockSpec...  30 us
    ppermute x9, waiting for transfers between devices, z_send(): lax.ppermute(value, 'fsdp', [(i, (i + 4 * step) % shards) for i in range(...  28.6 us
    pallas_call x1, Pallas kernels, attend_back(): pl.pallas_call(attend_back_kernel, grid=(pairs,), in_specs=[pl.BlockSpec(...  25.5 us
    ppermute x3, waiting for transfers between devices, x_swap(): return lax.ppermute(value, 'fsdp', [(i, i ^ 2) for i in range(shards)])  18.5 us
    ppermute x5, waiting for transfers between devices, send(): lax.ppermute(value, 'seq', [(i, (i + step) % splits) for i in range(split...  15.3 us
    ppermute x9, starting transfers between devices, z_send(): lax.ppermute(value, 'fsdp', [(i, (i + 4 * step) % shards) for i in range(...  15 us
  transfers between devices with their start and end apart: 34, of which 17 were waited for; matrix products, arithmetic and copies ran while one was open for 32% of the time, Pallas kernels for 14%

profile of v1, /device:TPU:0, one launch (start us, length us, event | category | flops | bytes accessed | tf_op | source)
XLA Modules:
  0.0 403.2 jit_solution(10446645779574853340)
XLA Ops:
  20.6 12.2 %collective-permute-done.3 = bf16[64,1024]{1,0:T(8,128)(2,1)S(1)} collective-permute-done((bf16[64,1024]{1,0:T(8,128)(2,1)}, bf16[64,1024]{1,0:T(8,128)(2,1)S(1)}, u32[]{:S(2)}, u32[]{:S(2)}) %collective-permute-start.3) | collective-permute-done | bytes 131104 | tf_op jit(solution)/shard_map/ppermute | solution.py:196
  43.3 9.6 %all-to-all-done = bf16[16,2,512]{2,1,0:T(2,128)(2,1)S(1)} async-done(((bf16[16,2,512]{2,1,0:T(2,128)(2,1)}), bf16[16,2,512]{2,1,0:T(2,128)(2,1)S(1)}, u32[]{:S(2)}, u32[]{:S(2)}) %all-to-all-start) | async-done | bytes 32800 | tf_op jit(solution)/shard_map/all_to_all | solution.py:231
  58.5 6.4 %all-to-all-done.1 = bf16[16,2,192]{2,1,0:T(2,128)(2,1)S(1)} async-done(((bf16[16,2,192]{2,1,0:T(2,128)(2,1)}), bf16[16,2,192]{2,1,0:T(2,128)(2,1)S(1)}, u32[]{:S(2)}, u32[]{:S(2)}) %all-to-all-start.1) | async-done | bytes 12320 | tf_op jit(solution)/shard_map/all_to_all | solution.py:239
  70.5 8.5 %convolution_convert_fusion.1.query_ref.all_ref = bf16[1024,1536]{1,0:T(8,128)(2,1)} fusion(bf16[1024,1536]{1,0:T(8,128)(2,1)} %all-gather.3.cloned.1.call-done, f32[1024]{0:T(1024)S(1)} %bitcast.184, f32[1024]{0:T(1024)S(1)} %bitcast.167, f32[1024]{0:T(1024)S(1)} %add_rsqrt_fusion, f32[1024]{0:T(1024)S(1)} %broadcast_multiply_fusion, ...), kind=kOutput, calls=%fused_computation.30 | convolution fusion | flops 3232235520 | bytes 8404992 | tf_op jit(solution)/shard_map/dot_general | solution.py:24
  79.0 14.7 %attend.2 = (bf16[512,512]{1,0:T(8,128)(2,1)}, f32[4,2,512]{2,1,0:T(2,128)}) custom-call(bf16[1024,1536]{1,0:T(8,128)(2,1)} %convolution_convert_fusion.1.query_ref.all_ref, bf16[1024,1536]{1,0:T(8,128)(2,1)} %convolution_convert_fusion.1.query_ref.all_ref), custom_call_target="tpu_custom_call" | custom-call | flops 4294967296 | bytes 3145728 | tf_op jit(solution)/shard_map/attend/pallas_call | solution.py:66
  95.4 15.3 %attend.3 = (bf16[512,512]{1,0:T(8,128)(2,1)}, f32[4,2,512]{2,1,0:T(2,128)}) custom-call(bf16[1024,1536]{1,0:T(8,128)(2,1)} %convolution_convert_fusion.1.query_ref.all_ref, bf16[1024,1536]{1,0:T(8,128)(2,1)} %convolution_convert_fusion.1.query_ref.all_ref), custom_call_target="tpu_custom_call" | custom-call | flops 4294967296 | bytes 3145728 | tf_op jit(solution)/shard_map/attend/pallas_call | solution.py:66
  118.3 24.1 %collective-permute-done.7 = bf16[512,1024]{1,0:T(8,128)(2,1)} collective-permute-done((bf16[512,1024]{1,0:T(8,128)(2,1)S(1)}, bf16[512,1024]{1,0:T(8,128)(2,1)}, u32[]{:S(2)}, u32[]{:S(2)}) %collective-permute-start.7) | collective-permute-done | bytes 1048608 | tf_op jit(solution)/shard_map/ppermute | solution.py:156
  142.5 5.0 %fusion.30 = f32[512,2048]{1,0:T(8,128)S(1)} fusion(bf16[512,1024]{1,0:T(8,128)(2,1)} %collective-permute-done.7, bf16[1024,4096]{1,0:T(8,128)(2,1)} %all-gather.5.cloned.1.call-done), kind=kOutput, calls=%fused_computation.48 | convolution fusion | flops 2147483648 | bytes 9437184 | tf_op jit(solution)/shard_map/dot_general | solution.py:24
  147.5 16.3 %collective-permute-done.9 = bf16[512,1024]{1,0:T(8,128)(2,1)} collective-permute-done((bf16[512,1024]{1,0:T(8,128)(2,1)}, bf16[512,1024]{1,0:T(8,128)(2,1)}, u32[]{:S(2)}, u32[]{:S(2)}) %collective-permute-start.9) | collective-permute-done | bytes 1048608 | tf_op jit(solution)/shard_map/ppermute | solution.py:156
  163.8 6.1 %fusion.16 = bf16[512,2048]{1,0:T(8,128)(2,1)S(1)} fusion(f32[512,2048]{1,0:T(8,128)S(1)} %fusion.30, bf16[1024,4096]{1,0:T(8,128)(2,1)S(1)} %copy-done.32, bf16[512,1024]{1,0:T(8,128)(2,1)} %collective-permute-done.9, f32[1024]{0:T(1024)S(1)} %bitcast.179), kind=kOutput, calls=%fused_computation.24 | convolution fusion | flops 2170028032 | bytes 11538432 | tf_op jit(solution)/shard_map/dot_general | solution.py:24
  178.3 6.1 %fusion.9 = bf16[512,2048]{1,0:T(8,128)(2,1)S(1)} fusion(f32[512,2048]{1,0:T(8,128)S(1)} %fusion.32, bf16[1024,4096]{1,0:T(8,128)(2,1)S(1)} %copy-done.32, f32[1024]{0:T(1024)S(1)} %bitcast.180, bf16[1,512,1024]{2,1,0:T(8,128)(2,1)} %param.11), kind=kOutput, calls=%fused_computation.17 | convolution fusion | flops 2170028032 | bytes 11538432 | tf_op jit(solution)/shard_map/dot_general | solution.py:24
  186.9 5.9 %add_convert_fusion.1 = bf16[1024,2048]{1,0:T(8,128)(2,1)} fusion(f32[1024,2048]{1,0:T(8,128)S(1)} %fusion.85, bf16[512,1024]{1,0:T(8,128)(2,1)} %collective-permute-done.7, bf16[512,2048]{1,0:T(8,128)(2,1)S(1)} %fusion.16), kind=kOutput, calls=%fused_computation.1 | convolution fusion | flops 2151677952 | bytes 15728640 | tf_op jit(solution)/shard_map/dot_general | solution.py:24
  192.9 5.2 %fusion.54 = f32[1024,2048]{1,0:T(8,128)S(1)} fusion(f32[1024]{0:T(1024)S(1)} %bitcast.181, bf16[1,512,1024]{2,1,0:T(8,128)(2,1)} %param.11, f32[512,2048]{1,0:T(8,128)} %copy-done.34), kind=kOutput, calls=%fused_computation.98 | convolution fusion | flops 2158493696 | bytes 13635584 | tf_op jit(solution)/shard_map/dot_general | solution.py:24
  198.0 5.5 %add_convert_fusion = bf16[1024,2048]{1,0:T(8,128)(2,1)} fusion(f32[1024,2048]{1,0:T(8,128)S(1)} %fusion.54, bf16[512,1024]{1,0:T(8,128)(2,1)} %collective-permute-done.9, f32[1024]{0:T(1024)S(1)} %bitcast.182, f32[512,2048]{1,0:T(8,128)S(1)} %copy-done.39), kind=kOutput, calls=%fused_computation | convolution fusion | flops 2162688000 | bytes 17829888 | tf_op jit(solution)/shard_map/dot_general | solution.py:24
  204.0 6.3 %fusion.46 = bf16[512,1024]{1,0:T(8,128)(2,1)S(1)} fusion(bf16[1024,4096]{1,0:T(8,128)(2,1)} %all-gather.5.cloned.1.call-done, f32[512,2048]{1,0:T(8,128)} %copy-done.38), kind=kOutput, calls=%fused_computation.83 | convolution fusion | flops 2157445120 | bytes 9437184 | tf_op jit(solution)/shard_map/dot_general | solution.py:24
  211.7 5.1 %fusion.24 = f32[512,1024]{1,0:T(8,128)S(1)} fusion(bf16[1024,4096]{1,0:T(8,128)(2,1)} %all-gather.5.cloned.1.call-done, f32[512,2048]{1,0:T(8,128)S(1)} %copy-done.35), kind=kOutput, calls=%fused_computation.42 | convolution fusion | flops 2156920832 | bytes 10485760 | tf_op jit(solution)/shard_map/dot_general | solution.py:24
  216.8 6.0 %multiply_reduce_fusion.1 = (f32[1024]{0:T(1024)S(1)}, f32[512]{0:T(512)S(1)}, f32[512]{0:T(512)S(1)}, f32[1024]{0:T(1024)S(1)}, f32[512,1024]{1,0:T(8,128)S(1)}) fusion(f32[512,1024]{1,0:T(8,128)S(1)} %get-tuple-element.34, f32[512]{0:T(512)S(1)} %add_rsqrt_fusion.1, f32[512]{0:T(512)S(1)} %broadcast_multiply_fusion.5, ...), kind=kOutput, calls=%fused_computation.61 | convolution fusion | flops 2153247744 | bytes 11554816 | tf_op jit(solution)/shard_map/dot_general | solution.py:24
  222.8 11.2 %collective-permute-done.8 = bf16[512,1024]{1,0:T(8,128)(2,1)S(1)} collective-permute-done((bf16[512,1024]{1,0:T(8,128)(2,1)S(1)}, bf16[512,1024]{1,0:T(8,128)(2,1)S(1)}, u32[]{:S(2)}, u32[]{:S(2)}) %collective-permute-start.8) | collective-permute-done | bytes 1048608 | tf_op jit(solution)/shard_map/ppermute | solution.py:159
  257.2 25.5 %attend_back.1 = bf16[1024,1536]{1,0:T(8,128)(2,1)} custom-call(bf16[1024,1536]{1,0:T(8,128)(2,1)} %convolution_convert_fusion.1.query_ref.all_ref, bf16[1024,512]{1,0:T(8,128)(2,1)} %pad_maximum_fusion.4.grad_ref, f32[4,2,1024]{2,1,0:T(2,128)} %pad_maximum_fusion.8.lse_ref, f32[4,2,1024]{2,1,0:T(2,128)} %bitcast.176), custom_call_target="tpu_custom_call" | custom-call | flops 21474836480 | bytes 6291456 | tf_op jit(solution)/shard_map/attend_back/pallas_call | solution.py:122
  282.7 7.8 %multiply_reduce_fusion = (f32[1024]{0:T(1024)S(1)}, f32[1024]{0:T(1024)S(1)}, f32[1024,1024]{1,0:T(8,128)}, f32[1024,1024]{1,0:T(8,128)S(1)}) fusion(f32[1024]{0:T(1024)S(1)} %add_rsqrt_fusion, f32[1024]{0:T(1024)S(1)} %broadcast_multiply_fusion, bf16[512,1024]{1,0:T(8,128)(2,1)S(1)} %copy-done.10, bf16[512,1024]{1,0:T(8,128)(2,1)S(1)} %bitcast.146, ...), kind=kOutput, calls=%fused_computation.25 | convolution fusion | flops 3230660608 | bytes 16793600 | tf_op jit(solution)/shard_map/dot_general | solution.py:24
  293.9 5.2 %convolution_convert_fusion = bf16[1024,1536]{1,0:T(8,128)(2,1)} fusion(bf16[1024,1536]{1,0:T(8,128)(2,1)S(1)} %copy-done.40, f32[1024]{0:T(1024)S(1)} %bitcast.185, f32[1024]{0:T(1024)S(1)} %bitcast.168, f32[1024]{0:T(1024)S(1)} %add_rsqrt_fusion, f32[1024]{0:T(1024)S(1)} %broadcast_multiply_fusion, bf16[512,1024]{1,0:T(8,128)(2,1)S(1)} %copy-done.10, ...), kind=kOutput, calls=%fused_computation.29 | convolution fusion | flops 3232235520 | bytes 8404992 | tf_op jit(solution)/shard_map/dot_general | solution.py:24
  321.1 12.2 %all-to-all-done.3 = bf16[16,2,512]{2,1,0:T(2,128)(2,1)S(1)} async-done(((bf16[16,2,512]{2,1,0:T(2,128)(2,1)}), bf16[16,2,512]{2,1,0:T(2,128)(2,1)S(1)}, u32[]{:S(2)}, u32[]{:S(2)}) %all-to-all-start.3) | async-done | bytes 32800 | tf_op jit(solution)/shard_map/all_to_all | solution.py:353
  347.1 18.5 %collective-permute-done.15 = bf16[4,64,1536]{2,1,0:T(8,128)(2,1)S(1)} collective-permute-done((bf16[4,64,1536]{2,1,0:T(8,128)(2,1)S(1)}, bf16[4,64,1536]{2,1,0:T(8,128)(2,1)S(1)}, u32[]{:S(2)}, u32[]{:S(2)}) %collective-permute-start.15) | collective-permute-done | bytes 786464 | tf_op jit(solution)/shard_map/ppermute | solution.py:193
  376.5 9.1 %collective-permute-done.17 = bf16[64,1536]{1,0:T(8,128)(2,1)S(1)} collective-permute-done((bf16[64,1536]{1,0:T(8,128)(2,1)S(1)}, bf16[64,1536]{1,0:T(8,128)(2,1)S(1)}, u32[]{:S(2)}, u32[]{:S(2)}) %collective-permute-start.17) | collective-permute-done | bytes 196640 | tf_op jit(solution)/shard_map/ppermute | solution.py:196
  (238 shorter events, 140.4 us)
Async XLA Ops:
  7.2 63.3 %all-gather.3.cloned.1.call-start = ((), (), s32[]{:S(2)}) async-start(), calls=%async_computation.6 | async-start | bytes 3342336 | tf_op jit(solution)/shard_map/all_gather | solution.py:247
  9.0 133.4 %all-gather.5.cloned.1.call-start = ((), (), s32[]{:S(2)}) async-start(), calls=%async_computation.7 | async-start | bytes 8912896 | tf_op jit(solution)/shard_map/all_gather | solution.py:249
  14.0 18.8 %collective-permute-start.4 = (bf16[64,1024]{1,0:T(8,128)(2,1)}, bf16[64,1024]{1,0:T(8,128)(2,1)S(1)}, u32[]{:S(2)}, u32[]{:S(2)}) collective-permute-start(bf16[64,1024]{1,0:T(8,128)(2,1)} %param.13), channel_id=1, source_target_pairs={{0,24},{2,26},{4,28},{6,30},{8,0},{10,2},{12,4},{14,6},{16,8},{18,... | collective-permute-start | bytes 393224 | tf_op jit(solution)/shard_map/ppermute | solution.py:196
  16.1 16.7 %collective-permute-start.3 = (bf16[64,1024]{1,0:T(8,128)(2,1)}, bf16[64,1024]{1,0:T(8,128)(2,1)S(1)}, u32[]{:S(2)}, u32[]{:S(2)}) collective-permute-start(bf16[64,1024]{1,0:T(8,128)(2,1)} %param.13), channel_id=1, source_target_pairs={{0,16},{2,18},{4,20},{6,22},{8,24},{10,26},{12,28},{14,30},{16,0},... | collective-permute-start | bytes 393224 | tf_op jit(solution)/shard_map/ppermute | solution.py:196
  32.9 32.1 %collective-permute-start.5 = (bf16[4,64,1024]{2,1,0:T(8,128)(2,1)S(1)}, bf16[4,64,1024]{2,1,0:T(8,128)(2,1)}, u32[]{:S(2)}, u32[]{:S(2)}) collective-permute-start(bf16[4,64,1024]{2,1,0:T(8,128)(2,1)S(1)} %bitcast_dynamic-update-slice_fusion), channel_id=1, source_target_pairs={{0,4},{2,6},{4,0},{6,2},{8,12},{10,14},{12,8},{14,10},{16,20},{18,... | collective-permute-start | bytes 1572872 | tf_op jit(solution)/shard_map/ppermute | solution.py:193
  41.7 25.4 %collective-permute-start = (bf16[512,1024]{1,0:T(8,128)(2,1)S(1)}, bf16[512,1024]{1,0:T(8,128)(2,1)S(1)}, u32[]{:S(2)}, u32[]{:S(2)}) collective-permute-start(bf16[512,1024]{1,0:T(8,128)(2,1)S(1)} %bitcast.142), channel_id=1, source_target_pairs={{1,0},{0,1},{3,2},{2,3},{5,4},{4,5},{7,6},{6,7},{9,8},{8,9},{11,10... | collective-permute-start | bytes 3145736 | tf_op jit(solution)/shard_map/ppermute | solution.py:156
  58.4 334.6 %reduce-scatter.5.cloned.1.call-start = ((), (), s32[]{:S(2)}) async-start(), calls=%async_computation.9 | async-start | bytes 4456448 | tf_op jit(solution)/shard_map/reduce_scatter | solution.py:297
  93.7 17.1 %collective-permute-start.1 = (bf16[512,512]{1,0:T(8,128)(2,1)}, bf16[512,512]{1,0:T(8,128)(2,1)S(1)}, u32[]{:S(2)}, u32[]{:S(2)}) collective-permute-start(bf16[512,512]{1,0:T(8,128)(2,1)} %get-tuple-element.16), channel_id=1, source_target_pairs={{0,1},{1,0},{2,3},{3,2},{4,5},{5,4},{6,7},{7,6},{8,9},{9,8},{10,11... | collective-permute-start | bytes 1572872 | tf_op jit(solution)/shard_map/ppermute | solution.py:159
  116.3 26.2 %collective-permute-start.7 = (bf16[512,1024]{1,0:T(8,128)(2,1)S(1)}, bf16[512,1024]{1,0:T(8,128)(2,1)}, u32[]{:S(2)}, u32[]{:S(2)}) collective-permute-start(bf16[512,1024]{1,0:T(8,128)(2,1)S(1)} %add_convert_fusion.4), channel_id=1, source_target_pairs={{1,0},{0,1},{3,2},{2,3},{5,4},{4,5},{7,6},{6,7},{9,8},{8,9},{11,10... | collective-permute-start | bytes 3145736 | tf_op jit(solution)/shard_map/ppermute | solution.py:156
  117.0 46.8 %collective-permute-start.9 = (bf16[512,1024]{1,0:T(8,128)(2,1)}, bf16[512,1024]{1,0:T(8,128)(2,1)}, u32[]{:S(2)}, u32[]{:S(2)}) collective-permute-start(bf16[512,1024]{1,0:T(8,128)(2,1)} %bitcast.23), channel_id=1, source_target_pairs={{1,0},{0,1},{3,2},{2,3},{5,4},{4,5},{7,6},{6,7},{9,8},{8,9},{11,10... | collective-permute-start | bytes 3145736 | tf_op jit(solution)/shard_map/ppermute | solution.py:156
  173.3 30.2 %collective-permute-start.10 = (bf16[512,1024]{1,0:T(8,128)(2,1)}, bf16[512,1024]{1,0:T(8,128)(2,1)}, u32[]{:S(2)}, u32[]{:S(2)}) collective-permute-start(bf16[512,1024]{1,0:T(8,128)(2,1)} %fusion.43), channel_id=1, source_target_pairs={{0,1},{1,0},{2,3},{3,2},{4,5},{5,4},{6,7},{7,6},{8,9},{9,8},{10,11... | collective-permute-start | bytes 3145736 | tf_op jit(solution)/shard_map/ppermute | solution.py:159
  203.5 191.2 %reduce-scatter.3.cloned.1.call-start = ((), (), s32[]{:S(2)}) async-start(), calls=%async_computation.8 | async-start | bytes 4456448 | tf_op jit(solution)/shard_map/reduce_scatter | solution.py:298
  210.3 23.8 %collective-permute-start.8 = (bf16[512,1024]{1,0:T(8,128)(2,1)S(1)}, bf16[512,1024]{1,0:T(8,128)(2,1)S(1)}, u32[]{:S(2)}, u32[]{:S(2)}) collective-permute-start(bf16[512,1024]{1,0:T(8,128)(2,1)S(1)} %fusion.46), channel_id=1, source_target_pairs={{0,1},{1,0},{2,3},{3,2},{4,5},{5,4},{6,7},{7,6},{8,9},{9,8},{10,11... | collective-permute-start | bytes 3145736 | tf_op jit(solution)/shard_map/ppermute | solution.py:159
  249.1 63.1 %collective-permute-start.20 = (bf16[8,64,1024]{2,1,0:T(8,128)(2,1)}, bf16[8,64,1024]{2,1,0:T(8,128)(2,1)}, u32[]{:S(2)}, u32[]{:S(2)}) collective-permute-start(bf16[8,64,1024]{2,1,0:T(8,128)(2,1)} %dynamic-slice_bitcast_fusion.1), channel_id=1, source_target_pairs={{0,2},{2,0},{4,6},{6,4},{8,10},{10,8},{12,14},{14,12},{16,18},{18,... | collective-permute-start | bytes 3145736 | tf_op jit(solution)/shard_map/ppermute | solution.py:190
  292.9 45.9 %collective-permute-start.12 = (bf16[512,1024]{1,0:T(8,128)(2,1)}, bf16[512,1024]{1,0:T(8,128)(2,1)S(1)}, u32[]{:S(2)}, u32[]{:S(2)}) collective-permute-start(bf16[512,1024]{1,0:T(8,128)(2,1)} %slice.99), channel_id=1, source_target_pairs={{0,1},{1,0},{2,3},{3,2},{4,5},{5,4},{6,7},{7,6},{8,9},{9,8},{10,11... | collective-permute-start | bytes 3145736 | tf_op jit(solution)/shard_map/ppermute | solution.py:159
  306.8 35.0 %collective-permute-start.14 = (bf16[8,64,1536]{2,1,0:T(8,128)(2,1)}, bf16[8,64,1536]{2,1,0:T(8,128)(2,1)}, u32[]{:S(2)}, u32[]{:S(2)}) collective-permute-start(bf16[8,64,1536]{2,1,0:T(8,128)(2,1)} %dynamic-slice_bitcast_fusion), channel_id=1, source_target_pairs={{0,2},{2,0},{4,6},{6,4},{8,10},{10,8},{12,14},{14,12},{16,18},{18,... | collective-permute-start | bytes 4718600 | tf_op jit(solution)/shard_map/ppermute | solution.py:190
  314.9 19.1 %collective-permute-start.21 = (bf16[4,64,1024]{2,1,0:T(8,128)(2,1)}, bf16[4,64,1024]{2,1,0:T(8,128)(2,1)S(1)}, u32[]{:S(2)}, u32[]{:S(2)}) collective-permute-start(bf16[4,64,1024]{2,1,0:T(8,128)(2,1)} %dynamic-slice_bitcast_fusion.3), channel_id=1, source_target_pairs={{0,4},{2,6},{4,0},{6,2},{8,12},{10,14},{12,8},{14,10},{16,20},{18,... | collective-permute-start | bytes 1572872 | tf_op jit(solution)/shard_map/ppermute | solution.py:193
  317.0 16.3 %all-to-all-start.3 = ((bf16[16,2,512]{2,1,0:T(2,128)(2,1)}), bf16[16,2,512]{2,1,0:T(2,128)(2,1)S(1)}, u32[]{:S(2)}, u32[]{:S(2)}) async-start(bf16[16,2,512]{2,1,0:T(2,128)(2,1)} %reshape.164), calls=%async_computation.3 | async-start | bytes 65536 | tf_op jit(solution)/shard_map/all_to_all | solution.py:353
  334.3 35.4 %collective-permute-start.22 = (bf16[64,1024]{1,0:T(8,128)(2,1)S(1)}, bf16[64,1024]{1,0:T(8,128)(2,1)S(1)}, u32[]{:S(2)}, u32[]{:S(2)}) collective-permute-start(bf16[64,1024]{1,0:T(8,128)(2,1)S(1)} %get-tuple-element.53), channel_id=1, source_target_pairs={{0,8},{2,10},{4,12},{6,14},{8,16},{10,18},{12,20},{14,22},{16,24},... | collective-permute-start | bytes 393224 | tf_op jit(solution)/shard_map/ppermute | solution.py:196
  335.8 34.3 %collective-permute-start.24 = (bf16[64,1024]{1,0:T(8,128)(2,1)S(1)}, bf16[64,1024]{1,0:T(8,128)(2,1)S(1)}, u32[]{:S(2)}, u32[]{:S(2)}) collective-permute-start(bf16[64,1024]{1,0:T(8,128)(2,1)S(1)} %get-tuple-element.54), channel_id=1, source_target_pairs={{0,24},{2,26},{4,28},{6,30},{8,0},{10,2},{12,4},{14,6},{16,8},{18,... | collective-permute-start | bytes 393224 | tf_op jit(solution)/shard_map/ppermute | solution.py:196
  338.2 32.0 %collective-permute-start.23 = (bf16[64,1024]{1,0:T(8,128)(2,1)S(1)}, bf16[64,1024]{1,0:T(8,128)(2,1)S(1)}, u32[]{:S(2)}, u32[]{:S(2)}) collective-permute-start(bf16[64,1024]{1,0:T(8,128)(2,1)S(1)} %get-tuple-element.55), channel_id=1, source_target_pairs={{0,16},{2,18},{4,20},{6,22},{8,24},{10,26},{12,28},{14,30},{16,0},... | collective-permute-start | bytes 393224 | tf_op jit(solution)/shard_map/ppermute | solution.py:196
  343.8 21.7 %collective-permute-start.15 = (bf16[4,64,1536]{2,1,0:T(8,128)(2,1)S(1)}, bf16[4,64,1536]{2,1,0:T(8,128)(2,1)S(1)}, u32[]{:S(2)}, u32[]{:S(2)}) collective-permute-start(bf16[4,64,1536]{2,1,0:T(8,128)(2,1)S(1)} %dynamic-slice_bitcast_fusion.2), channel_id=1, source_target_pairs={{0,4},{2,6},{4,0},{6,2},{8,12},{10,14},{12,8},{14,10},{16,20},{18,... | collective-permute-start | bytes 2359304 | tf_op jit(solution)/shard_map/ppermute | solution.py:193
  369.7 15.9 %collective-permute-start.17 = (bf16[64,1536]{1,0:T(8,128)(2,1)S(1)}, bf16[64,1536]{1,0:T(8,128)(2,1)S(1)}, u32[]{:S(2)}, u32[]{:S(2)}) collective-permute-start(bf16[64,1536]{1,0:T(8,128)(2,1)S(1)} %get-tuple-element.52), channel_id=1, source_target_pairs={{0,16},{2,18},{4,20},{6,22},{8,24},{10,26},{12,28},{14,30},{16,0},... | collective-permute-start | bytes 589832 | tf_op jit(solution)/shard_map/ppermute | solution.py:196
  370.3 16.9 %collective-permute-start.25 = (bf16[64,1024]{1,0:T(8,128)(2,1)S(1)}, bf16[64,1024]{1,0:T(8,128)(2,1)S(1)}, u32[]{:S(2)}, u32[]{:S(2)}) collective-permute-start(bf16[64,1024]{1,0:T(8,128)(2,1)S(1)} %fusion.64), channel_id=1, source_target_pairs={{1,0},{0,1},{3,2},{2,3},{5,4},{4,5},{7,6},{6,7},{9,8},{8,9},{11,10... | collective-permute-start | bytes 393224 | tf_op jit(solution)/shard_map/ppermute | solution.py:156
  (52 other events, 829.1 us)
Sparse Core Ops, SparseCore 0:
  10.9 51.6 all-gather.2
  65.3 75.9 all-gather.4
  203.7 71.9 reduce-scatter.4
  279.8 82.9 reduce-scatter.2

commit v2 on v1

--- a/solution.py
+++ b/solution.py
@@ -14,6 +14,8 @@
 SCALE2 = HD**-0.5 * LOG2E
 VMEM = 56 * 1024 * 1024
 CHUNK = 256
+ROOT = 0.7978845608028654
+CUBE = 0.044715
 
 NT = (((1,), (1,)), ((), ()))
 TN = (((0,), (0,)), ((), ()))
@@ -88,6 +90,68 @@
     )(qkv, qkv)
 
 
+def feed_kernel(aliased, hidden_ref, grad_ref, up_ref, down_ref, *rest):
+    act_ref, grad_up_ref, branch_ref, part_ref, branch_acc, part_acc = rest[2 * aliased :]
+    step = pl.program_id(0)
+    up_weights, down_weights = up_ref[...], down_ref[...]
+    value = mm(hidden_ref[...], up_weights)
+    grad_act = mm(grad_ref[...], down_weights)
+    square = value * value
+    tanh = jnp.tanh(ROOT * value * (1.0 + CUBE * square))
+    half = 0.5 * (1.0 + tanh)
+    act = (value * half).astype(jnp.bfloat16)
+    slope = half + (0.5 * ROOT) * value * (1.0 - tanh * tanh) * (1.0 + 3.0 * CUBE * square)
+    grad_up = (grad_act * slope).astype(jnp.bfloat16)
+    act_ref[...] = act
+    grad_up_ref[...] = grad_up
+    part = mm(grad_up, up_weights, NT)
+    branch = mm(act, down_weights, NT)
+
+    @pl.when(step == 0)
+    def _():
+        part_acc[...] = part
+        branch_acc[...] = branch
+
+    @pl.when(step > 0)
+    def _():
+        part_acc[...] += part
+        branch_acc[...] += branch
+
+    @pl.when(step == pl.num_programs(0) - 1)
+    def _():
+        part_ref[...] = part_acc[...].astype(part_ref.dtype)
+        branch_ref[...] = branch_acc[...].astype(branch_ref.dtype)
+
+
+def feed(hidden, grads_all, up_full, down_full, piece, buffers, out_type):
+    tokens, width = hidden.shape
+    units = up_full.shape[1]
+    block = min(512, units)
+    length = grads_all.shape[0]
+    weights = pl.BlockSpec((width, block), lambda j: (0, j))
+    rows = pl.BlockSpec((tokens, block), lambda j: (piece, j))
+    whole = pl.BlockSpec((tokens, width), lambda j: (0, 0))
+    aliased = buffers is not None
+    return pl.pallas_call(
+        partial(feed_kernel, int(aliased)),
+        grid=(units // block,),
+        in_specs=[whole, pl.BlockSpec((tokens, width), lambda j: (piece, 0)), weights, weights]
+        + [pl.BlockSpec(memory_space=pl.ANY)] * (2 * aliased),
+        out_specs=[rows, rows, whole, whole],
+        out_shape=[jax.ShapeDtypeStruct((length, units), jnp.bfloat16)] * 2
+        + [jax.ShapeDtypeStruct((tokens, width), out_type)] * 2,
+        scratch_shapes=[pltpu.VMEM((tokens, width), jnp.float32)] * 2,
+        input_output_aliases={4: 0, 5: 1} if aliased else {},
+        compiler_params=pltpu.CompilerParams(vmem_limit_bytes=VMEM),
+        cost_estimate=pl.CostEstimate(
+            flops=8 * tokens * width * units,
+            bytes_accessed=4 * width * units + 8 * tokens * width + 4 * tokens * units,
+            transcendentals=tokens * units,
+        ),
+        name="feed",
+    )(hidden, grads_all, up_full, down_full, *(buffers or ()))
+
+
 def attend_back_kernel(all_ref, grad_ref, lse_ref, delta_ref, out_ref, key_acc, value_acc):
     length = all_ref.shape[0]
     scaling = HD**-0.5
@@ -116,17 +180,17 @@
         out_ref[:, base + 2 * HD : base + 3 * HD] = value_acc[...].astype(jnp.bfloat16)
 
 
-def attend_back(qkv, grad_attn, lse, delta):
-    length, columns = qkv.shape
-    pairs = columns // (6 * HD)
+def attend_back(qkv, grad_attn, lse, delta, first, pairs):
+    length = qkv.shape[0]
+    columns = pairs * 6 * HD
     return pl.pallas_call(
         attend_back_kernel,
         grid=(pairs,),
         in_specs=[
-            pl.BlockSpec((length, 6 * HD), lambda p: (0, p)),
-            pl.BlockSpec((length, 2 * HD), lambda p: (0, p)),
-            pl.BlockSpec((1, 2, length), lambda p: (p, 0, 0)),
-            pl.BlockSpec((1, 2, length), lambda p: (p, 0, 0)),
+            pl.BlockSpec((length, 6 * HD), lambda p: (0, first + p)),
+            pl.BlockSpec((length, 2 * HD), lambda p: (0, first + p)),
+            pl.BlockSpec((1, 2, length), lambda p: (first + p, 0, 0)),
+            pl.BlockSpec((1, 2, length), lambda p: (first + p, 0, 0)),
         ],
         out_specs=pl.BlockSpec((length, 6 * HD), lambda p: (0, p)),
         out_shape=jax.ShapeDtypeStruct((length, columns), jnp.bfloat16),
@@ -200,32 +264,56 @@
             [jnp.where(at == 0, mine, other), jnp.where(at == 0, other, mine)], 1
         )
 
-    def gather_rows(shard):
-        rows, cols = shard.shape
-        line = jnp.zeros((depth, rows, cols), shard.dtype)
-        for step in range(depth):
-            piece = z_send(shard, step) if step else shard
-            line = lax.dynamic_update_slice_in_dim(
-                line, piece[None], (z_at - step) % depth, 0
-            )
-        plane = two(line, x_swap(line), x_at).reshape(2 * depth, rows, cols)
-        return two(plane, core_swap(plane), core_at).reshape(shards * rows, cols)
+    def gather_z(shard):
+        return [shard] + [z_send(shard, step) for step in range(1, depth)]
+
+    def gather_x(pieces):
+        rows, cols = pieces[0].shape
+        line = jnp.zeros((depth, rows, cols), pieces[0].dtype)
+        for step, piece in enumerate(pieces):
+            line = lax.dynamic_update_slice_in_dim(line, piece[None], (z_at - step) % depth, 0)
+        return line, x_swap(line)
+
+    def gather_core(pair):
+        rows, cols = pair[0].shape[1:]
+        plane = two(*pair, x_at).reshape(2 * depth, rows, cols)
+        return plane, core_swap(plane)
+
+    def gather_end(pair):
+        rows, cols = pair[0].shape[1:]
+        return two(*pair, core_at).reshape(shards * rows, cols)
 
     def halve(value, at, swap):
         mine = lax.dynamic_index_in_dim(value, at, 1, keepdims=False)
         other = lax.dynamic_index_in_dim(value, 1 - at, 1, keepdims=False)
-        return (mine.astype(wide) + swap(other).astype(wide)).astype(low)
-
-    def scatter_rows(value):
+        return mine, swap(other)
+
+    def add(pair):
+        return (pair[0].astype(wide) + pair[1].astype(wide)).astype(low)
+
+    def scatter_core(value):
         rows, cols = value.shape[0] // shards, value.shape[1]
-        value = halve(value.reshape(2 * depth, 2, rows, cols), core_at, core_swap)
-        value = halve(value.reshape(depth, 2, rows, cols), x_at, x_swap)
-        total = lax.dynamic_index_in_dim(value, z_at, 0, keepdims=False).astype(wide)
+        return halve(value.reshape(2 * depth, 2, rows, cols), core_at, core_swap)
+
+    def scatter_x(pair):
+        rows, cols = pair[0].shape[1:]
+        return halve(add(pair).reshape(depth, 2, rows, cols), x_at, x_swap)
+
+    def scatter_z(pair):
+        value = add(pair)
+        pieces = [lax.dynamic_index_in_dim(value, z_at, 0, keepdims=False)]
         for step in range(1, depth):
             piece = lax.dynamic_index_in_dim(value, (z_at + step) % depth, 0, keepdims=False)
-            total = total + z_send(piece, step).astype(wide)
+            pieces.append(z_send(piece, step))
+        return pieces
+
+    def scatter_end(pieces):
+        total = pieces[0].astype(wide)
+        for piece in pieces[1:]:
+            total = total + piece.astype(wide)
         return total
 
+    after = lax.optimization_barrier
     own_latents, own_cotangent = latents[0], cotangent[0]
     cond_act, silu_back = jax.vjp(jax.nn.silu, cond.astype(wide))
     cond_all = lax.all_to_all(
@@ -235,32 +323,37 @@
         concat_axis=0,
         tiled=True,
     )
+    cond_all, out_shard, up_shard = after((cond_all, w_out, w_up))
+    out_pieces, up_pieces = gather_z(out_shard), gather_z(up_shard)
     mod_cols = (mm(cond_all, w_ada) + b_ada.astype(wide)).astype(low)
     modulation = lax.all_to_all(
         mod_cols, "fsdp", split_axis=0, concat_axis=1, tiled=True
     ).astype(wide)
+    modulation, out_pieces, up_pieces = after((modulation, out_pieces, up_pieces))
+    out_pair, up_pair = gather_x(out_pieces), gather_x(up_pieces)
     shift_one, scale_one, gate_one, shift_two, scale_two, gate_two = [
         modulation[:, position * width : (position + 1) * width] for position in range(6)
     ]
     columns = heads * 3 * HD
     qkv_shard = lax.dynamic_slice_in_dim(w_qkv, me * columns, columns, 1)
     qkv_half = lax.all_gather(qkv_shard, "fsdp", axis=0, tiled=True)
-    out_full = gather_rows(w_out)
-    up_down = lax.all_gather(jnp.concatenate([w_up, w_down.T], 1), "fsdp", axis=0, tiled=True)
-    hidden_units = w_up.shape[1]
-    up_full, down_full = up_down[:, :hidden_units], up_down[:, hidden_units:]
+    down_full = lax.all_gather(w_down.T, "fsdp", axis=0, tiled=True)
 
     latents_all = jnp.concatenate(everyone(own_latents), 0)
-    cotangents = everyone(own_cotangent)
-    grad_rows = [(gate_two * value.astype(wide)).astype(low) for value in cotangents]
+    cotangent_all = jnp.concatenate(everyone(own_cotangent), 0)
+    grad_rows = (gate_two * cotangent_all.astype(wide)).astype(low)
 
     normed_all, inverse_all = normalize(latents_all.astype(wide))
     hidden_one = (normed_all * (1.0 + scale_one) + shift_one).astype(low)
     qkv = mm(hidden_one, qkv_half).astype(low)
     attn_peers, lse_peers = attend(qkv, tokens, 1, splits - 1)
+    attn_peers, out_pair = after((attn_peers, out_pair))
+    out_pair = gather_core(out_pair)
     peer_rows = [attn_peers[r * tokens : (r + 1) * tokens] for r in range(splits - 1)]
     arrived = [send(value, r + 1) for r, value in enumerate(peer_rows)]
     attn_own, lse_own = attend(qkv, tokens, 0, 1)
+    attn_own, out_pair, up_pair = after((attn_own, out_pair, up_pair))
+    out_full, up_pair = gather_end(out_pair), gather_core(up_pair)
     attn_rows = in_order([attn_own] + arrived[::-1], 1)
     branch_one = mm(attn_rows, out_full)
     inputs = own_latents.astype(wide)
@@ -269,16 +362,23 @@
     hidden_two = (normed_two * (1.0 + scale_two) + shift_two).astype(low)
 
     hidden_pieces = everyone(hidden_two)
-    branch_parts, grad_parts, term_up, term_down = [], [], 0.0, 0.0
-    for hidden, grads in zip(hidden_pieces, grad_rows):
-        up_values = mm(hidden, up_full)
-        activated, gelu_back = jax.vjp(partial(jax.nn.gelu, approximate=True), up_values)
-        activated = activated.astype(low)
-        grad_up = gelu_back(mm(grads, down_full))[0].astype(low)
-        grad_parts.append(mm(grad_up, up_full, NT))
-        branch_parts.append(mm(activated, down_full, NT))
-        term_up = term_up + mm(hidden, grad_up, TN)
-        term_down = term_down + mm(grads, activated, TN)
+    up_full = gather_end(up_pair)
+    buffers, grad_parts, branch_parts = None, [], []
+    for piece in range(splits):
+        act, grad_up, branch_part, grad_part = feed(
+            hidden_pieces[piece],
+            grad_rows,
+            up_full,
+            down_full,
+            piece,
+            buffers,
+            low if piece else wide,
+        )
+        buffers = (act, grad_up)
+        grad_parts.append(grad_part)
+        branch_parts.append(branch_part)
+        if piece + 1 < splits:
+            hidden_pieces[piece + 1], buffers = after((hidden_pieces[piece + 1], buffers))
 
     def send_parts(parts):
         return [send(parts[step].astype(low), step) for step in range(1, splits)]
@@ -288,17 +388,17 @@
             own = own + value.astype(wide)
         return own
 
-    term_up, term_down = term_up.astype(low), term_down.astype(low)
     grad_sent = send_parts(grad_parts)
-    branch_sent = send_parts(branch_parts)
-    grad_sent, term_up, term_down = lax.optimization_barrier((grad_sent, term_up, term_down))
+    term_up = mm(jnp.concatenate(hidden_pieces, 0), grad_up, TN).astype(low)
+    up_pair = scatter_core(term_up)
+    term_down = mm(grad_rows, act, TN).astype(low)
+    grad_w_down = lax.psum_scatter(term_down, "fsdp", scatter_dimension=0, tiled=True)
+    grad_sent, up_pair, term_down, branch_parts = after(
+        (grad_sent, up_pair, term_down, branch_parts)
+    )
+    up_pair = scatter_x(up_pair)
     grad_hidden_two = add_parts(grad_parts[0], grad_sent)
-    branch_two = add_parts(branch_parts[0], branch_sent)
-    grad_w_down = lax.psum_scatter(term_down, "fsdp", scatter_dimension=0, tiled=True)
-    grad_w_up = lax.psum_scatter(term_up, "fsdp", scatter_dimension=0, tiled=True)
     grad_mixed = own_cotangent.astype(wide)
-    mixed = (middle + gate_two * branch_two).astype(low)
-    grad_gate_two = jnp.sum(grad_mixed * branch_two, 0)
     grad_shift_two = jnp.sum(grad_hidden_two, 0)
     grad_scale_two = jnp.sum(grad_hidden_two * normed_two, 0)
     grad_middle = grad_mixed + norm_grad(
@@ -314,22 +414,55 @@
         for r in range(splits)
     ]
     grad_arrived = [send(grad_pieces[r], r) for r in range(1, splits)]
+    term_out = mm(attn_rows, grad_branch_one, TN).astype(low)
+    out_pair = scatter_core(term_out)
+    grad_arrived, branch_parts, up_pair, out_pair = after(
+        (grad_arrived, branch_parts, up_pair, out_pair)
+    )
+    branch_sent = send_parts(branch_parts)
+    up_pieces, out_pair = scatter_z(up_pair), scatter_x(out_pair)
     grad_heads = jnp.concatenate([grad_pieces[0]] + grad_arrived[::-1], 0)
     attn_all = jnp.concatenate([attn_own, attn_peers], 0)
     lse = jnp.concatenate([lse_own, lse_peers], 2)
     delta = jnp.sum(
         (grad_heads.astype(wide) * attn_all.astype(wide)).reshape(-1, heads // 2, 2, HD), -1
     ).transpose(1, 2, 0)
-    grad_qkv = attend_back(qkv, grad_heads, lse, delta)
-    term_out = mm(attn_rows, grad_branch_one, TN)
-    grad_w_out = scatter_rows(term_out.astype(low)).astype(low)
-    term_qkv = mm(hidden_one, grad_qkv, TN)
-    grad_w_qkv = scatter_rows(term_qkv.astype(low)).astype(low)
-    hidden_grad_all = mm(grad_qkv, qkv_half, NT)
+    pairs = heads // 2
+    groups = 2 if pairs % 2 == 0 else 1
+    each = pairs // groups
+    grad_qkv, qkv_pairs = [], []
+    for group in range(groups):
+        grad_qkv.append(attend_back(qkv, grad_heads, lse, delta, group * each, each))
+        term_qkv = mm(hidden_one, grad_qkv[-1], TN).astype(low)
+        pair = scatter_core(term_qkv)
+        if group + 1 < groups:
+            pair, grad_heads, out_pair = after((pair, grad_heads, out_pair))
+            out_pieces = scatter_z(out_pair)
+            pair = scatter_x(pair)
+        else:
+            pair, grad_qkv = after((pair, grad_qkv))
+        qkv_pairs.append(pair)
+    if groups == 1:
+        out_pieces = scatter_z(out_pair)
+    size = each * 6 * HD
+    hidden_grad_all = sum(
+        mm(value, qkv_half[:, group * size : (group + 1) * size], NT)
+        for group, value in enumerate(grad_qkv)
+    )
     grad_shift_one = jnp.sum(hidden_grad_all, 0)
     grad_scale_one = jnp.sum(hidden_grad_all * normed_all, 0)
     hidden_parts = [hidden_grad_all[r * tokens : (r + 1) * tokens] for r in range(splits)]
-    grad_hidden_one = add_parts(hidden_parts[0], send_parts(hidden_parts))
+    hidden_sent = send_parts(hidden_parts)
+    qkv_pairs[-1] = scatter_x(qkv_pairs[-1])
+    grad_w_up = scatter_end(up_pieces)
+    grad_w_out = scatter_end(out_pieces).astype(low)
+    grad_w_qkv = jnp.concatenate(
+        [scatter_end(scatter_z(pair)).astype(low) for pair in qkv_pairs], 1
+    )
+    branch_two = add_parts(branch_parts[0], branch_sent)
+    mixed = (middle + gate_two * branch_two).astype(low)
+    grad_gate_two = jnp.sum(grad_mixed * branch_two, 0)
+    grad_hidden_one = add_parts(hidden_parts[0], hidden_sent)
     grad_latents = grad_middle + norm_grad(
         normed_all[:tokens], inverse_all[:tokens], grad_hidden_one * (1.0 + scale_one)
     )
@@ -361,7 +494,7 @@
         grad_cond,
         grad_w_qkv,
         grad_w_out,
-        grad_w_up.astype(wide),
+        grad_w_up,
         grad_w_down.T.astype(wide),
         grad_w_ada,
         grad_b_ada,

time: 407 us -> 485 us (1.19)
  matrix products: 90 us -> 45.8 us
  waiting for transfers between devices: 140 us -> 174 us
  Pallas kernels: 55.5 us -> 89.1 us
  local copies, waits for them, and re-layouts: 20.3 us -> 39 us
  other arithmetic: 36 us -> 53.7 us
  blocking collectives: 0 us -> 13.8 us
    dot_general x21 -> x13, matrix products: 90 us -> 45.8 us  [mm(): return lax.dot_general(a, b, dims, preferred_element_type=jnp.float32)]
    ppermute x9 -> x18, waiting for transfers between devices: 28.6 us -> 61.7 us  [z_send(): lax.ppermute(value, 'fsdp', [(i, (i + 4 * step) % shards) for i in range(...]
    pallas_call x0 -> x2, Pallas kernels: none -> 32 us  [feed(): pl.pallas_call(partial(feed_kernel, int(aliased)), grid=(units // block,)...]
    all_to_all x1, waiting for transfers between devices: 6.38 us -> 38.1 us  [per_device(): lax.all_to_all(mod_cols, 'fsdp', split_axis=0, concat_axis=1, tiled=True)]
    ppermute x3 -> x6, waiting for transfers between devices: 18.5 us -> 0.02 us  [x_swap(): return lax.ppermute(value, 'fsdp', [(i, i ^ 2) for i in range(shards)])]
    all_to_all x0 -> x1, blocking collectives: none -> 13.8 us  [per_device(): lax.all_to_all(jnp.broadcast_to(cond_act.astype(low), (shards, width)), '...]
    all_to_all x1 -> x0, waiting for transfers between devices: 9.61 us -> none  [per_device(): lax.all_to_all(jnp.broadcast_to(cond_act.astype(low), (shards, width)), '...]
    all_to_all x1, waiting for transfers between devices: 12.2 us -> 4.43 us  [per_device(): lax.all_to_all(cond_term, 'fsdp', split_axis=0, concat_axis=0, tiled=True)]
  transfers between devices with their start and end apart: 34 -> 47, of which waited for: 17 -> 18; matrix products, arithmetic and copies ran while one was open for 32% -> 22% of each run, Pallas kernels for 14% -> 12%
where the time goes in v2:
time: 485 us; the launch traced here: 479 us
  waiting for transfers between devices  174 us (36%)
  Pallas kernels  89.1 us (18%)
  other arithmetic  53.7 us (11%)
  starting transfers between devices  48.3 us (10%)
  matrix products  45.8 us (9%)
  local copies, waits for them, and re-layouts  39 us (8%)
  between operations  15.3 us (3%)
  blocking collectives  13.8 us (3%)
    ppermute x18, waiting for transfers between devices, z_send(): lax.ppermute(value, 'fsdp', [(i, (i + 4 * step) % shards) for i in range(...  61.7 us
    dot_general x13, matrix products, mm(): return lax.dot_general(a, b, dims, preferred_element_type=jnp.float32)  45.8 us
    ppermute x6, waiting for transfers between devices, fetch(): lax.ppermute(value, 'seq', [((i + step) % splits, i) for i in range(split...  41.8 us
    all_to_all x1, waiting for transfers between devices, per_device(): lax.all_to_all(mod_cols, 'fsdp', split_axis=0, concat_axis=1, tiled=True)  38.1 us
    pallas_call x2, Pallas kernels, feed(): pl.pallas_call(partial(feed_kernel, int(aliased)), grid=(units // block,)...  32 us
    pallas_call x2, Pallas kernels, attend(): pl.pallas_call(attend_kernel, grid=(pairs, count), in_specs=[pl.BlockSpec...  29.3 us
    pallas_call x2, Pallas kernels, attend_back(): pl.pallas_call(attend_back_kernel, grid=(pairs,), in_specs=[pl.BlockSpec(...  27.7 us
    ppermute x5, waiting for transfers between devices, send(): lax.ppermute(value, 'seq', [(i, (i + step) % splits) for i in range(split...  23 us
  transfers between devices with their start and end apart: 47, of which 18 were waited for; matrix products, arithmetic and copies ran while one was open for 22% of the time, Pallas kernels for 12%

profile of v2, /device:TPU:0, one launch (start us, length us, event | category | flops | bytes accessed | tf_op | source)
XLA Modules:
  0.0 478.5 jit_solution(18208737777228203524)
XLA Ops:
  11.2 13.8 %all_to_all.47 = bf16[16,2,512]{2,1,0:T(2,128)(2,1)S(1)} all-to-all(bf16[16,2,512]{2,1,0:T(2,128)(2,1)S(1)} %reshape.182), channel_id=1, replica_groups=mesh['fsdp'=16,'seq'=2] {'fsdp'}, dimensions={0} | all-to-all | bytes 65536 | tf_op jit(solution)/shard_map/all_to_all | solution.py:319
  42.2 38.1 %all-to-all-done.1 = bf16[16,2,192]{2,1,0:T(2,128)(2,1)S(1)} async-done(((bf16[16,2,192]{2,1,0:T(2,128)(2,1)}), bf16[16,2,192]{2,1,0:T(2,128)(2,1)S(1)}, u32[]{:S(2)}, u32[]{:S(2)}) %all-to-all-start.1) | async-done | bytes 12320 | tf_op jit(solution)/shard_map/all_to_all | solution.py:329
  95.7 10.8 %collective-permute-done.6 = bf16[512,1024]{1,0:T(8,128)(2,1)S(1)} collective-permute-done((bf16[512,1024]{1,0:T(8,128)(2,1)S(1)}, bf16[512,1024]{1,0:T(8,128)(2,1)S(1)}, u32[]{:S(2)}, u32[]{:S(2)}) %collective-permute-start.6) | collective-permute-done | bytes 1048608 | tf_op jit(solution)/shard_map/ppermute | solution.py:220
  107.5 8.0 %convolution_convert_fusion.query_ref.all_ref = bf16[1024,1536]{1,0:T(8,128)(2,1)} fusion(bf16[1024,1536]{1,0:T(8,128)(2,1)} %all-gather.3.cloned.1.call-done, f32[1024]{0:T(1024)S(1)} %bitcast.237, f32[1024]{0:T(1024)S(1)} %bitcast.224, f32[1024]{0:T(1024)S(1)} %add_rsqrt_fusion, f32[1024]{0:T(1024)S(1)} %broadcast_multiply_fusion, ...), kind=kOutput, calls=%fused_computation.10 | convolution fusion | flops 3232235520 | bytes 8404992 | tf_op jit(solution)/shard_map/dot_general | solution.py:26
  115.5 14.7 %attend.2 = (bf16[512,512]{1,0:T(8,128)(2,1)}, f32[4,2,512]{2,1,0:T(2,128)}) custom-call(bf16[1024,1536]{1,0:T(8,128)(2,1)} %convolution_convert_fusion.query_ref.all_ref, bf16[1024,1536]{1,0:T(8,128)(2,1)} %convolution_convert_fusion.query_ref.all_ref), custom_call_target="tpu_custom_call" | custom-call | flops 4294967296 | bytes 3145728 | tf_op jit(solution)/shard_map/attend/pallas_call | solution.py:68
  136.5 14.5 %attend.3 = (bf16[512,512]{1,0:T(8,128)(2,1)}, f32[4,2,512]{2,1,0:T(2,128)}) custom-call(bf16[1024,1536]{1,0:T(8,128)(2,1)} %convolution_convert_fusion.query_ref.all_ref, bf16[1024,1536]{1,0:T(8,128)(2,1)} %convolution_convert_fusion.query_ref.all_ref), custom_call_target="tpu_custom_call" | custom-call | flops 4294967296 | bytes 3145728 | tf_op jit(solution)/shard_map/attend/pallas_call | solution.py:68
  164.7 16.6 %feed.2 = (bf16[1024,2048]{1,0:T(8,128)(2,1)}, bf16[1024,2048]{1,0:T(8,128)(2,1)}, f32[512,1024]{1,0:T(8,128)}, f32[512,1024]{1,0:T(8,128)}) custom-call(bf16[512,1024]{1,0:T(8,128)(2,1)} %add_convert_fusion.5.hidden_ref, bf16[1024,1024]{1,0:T(8,128)(2,1)} %multiply_convert_fusion.grad_ref, bf16[1024,2048]{1,0:T(8,128)(2,1)} %bitcast.197, ...), custom_call_target="tpu_custom_call" | custom-call | flops 8589934592 | bytes 16777216 | tf_op jit(solution)/shard_map/feed/pallas_call | solution.py:135
  181.3 5.8 %collective-permute-done.13.hidden_ref = bf16[512,1024]{1,0:T(8,128)(2,1)} collective-permute-done((bf16[512,1024]{1,0:T(8,128)(2,1)}, bf16[512,1024]{1,0:T(8,128)(2,1)}, u32[]{:S(2)}, u32[]{:S(2)}) %collective-permute-start.13) | collective-permute-done | bytes 1048608 | tf_op jit(solution)/shard_map/ppermute | solution.py:220
  187.1 15.4 %feed.3 = (bf16[1024,2048]{1,0:T(8,128)(2,1)}, bf16[1024,2048]{1,0:T(8,128)(2,1)}, bf16[512,1024]{1,0:T(8,128)(2,1)}, bf16[512,1024]{1,0:T(8,128)(2,1)}) custom-call(bf16[512,1024]{1,0:T(8,128)(2,1)} %collective-permute-done.13.hidden_ref, bf16[1024,1024]{1,0:T(8,128)(2,1)} %multiply_convert_fusion.grad_ref, ...), custom_call_target="tpu_custom_call", output_to_operand_aliasing={{0}: (4, {}), {1}: (5, {})} | custom-call | flops 8589934592 | bytes 16777216 | tf_op jit(solution)/shard_map/feed/pallas_call | solution.py:135
  202.5 7.4 %convolution_convert_fusion.2 = bf16[1024,2048]{1,0:T(8,128)(2,1)S(1)} fusion(bf16[1024,2048]{1,0:T(8,128)(2,1)} %get-tuple-element.94, bf16[512,1024]{1,0:T(8,128)(2,1)} %collective-permute-done.13.hidden_ref, bf16[512,1024]{1,0:T(8,128)(2,1)} %add_convert_fusion.5.hidden_ref), kind=kOutput, calls=%fused_computation.12 | convolution fusion | flops 4301258752 | bytes 10485760 | tf_op jit(solution)/shard_map/dot_general | solution.py:26
  212.8 9.4 %convolution_convert_fusion.1 = bf16[1024,2048]{1,0:T(8,128)(2,1)} fusion(bf16[1024,1024]{1,0:T(8,128)(2,1)} %multiply_convert_fusion.grad_ref, bf16[1024,2048]{1,0:T(8,128)(2,1)} %get-tuple-element.95), kind=kOutput, calls=%fused_computation.11 | convolution fusion | flops 4297064448 | bytes 10485760 | tf_op jit(solution)/shard_map/dot_general | solution.py:26
  222.2 15.9 %collective-permute-done.14 = bf16[512,1024]{1,0:T(8,128)(2,1)} collective-permute-done((bf16[512,1024]{1,0:T(8,128)(2,1)}, bf16[512,1024]{1,0:T(8,128)(2,1)}, u32[]{:S(2)}, u32[]{:S(2)}) %collective-permute-start.14) | collective-permute-done | bytes 1048608 | tf_op jit(solution)/shard_map/ppermute | solution.py:223
  261.2 7.0 %collective-permute-done.16 = bf16[512,512]{1,0:T(8,128)(2,1)} collective-permute-done((bf16[512,512]{1,0:T(8,128)(2,1)}, bf16[512,512]{1,0:T(8,128)(2,1)}, u32[]{:S(2)}, u32[]{:S(2)}) %collective-permute-start.16) | collective-permute-done | bytes 524320 | tf_op jit(solution)/shard_map/ppermute | solution.py:223
  273.9 14.0 %attend_back.2 = bf16[1024,768]{1,0:T(8,128)(2,1)} custom-call(bf16[1024,1536]{1,0:T(8,128)(2,1)} %convolution_convert_fusion.query_ref.all_ref, bf16[1024,512]{1,0:T(8,128)(2,1)} %pad_maximum_fusion.6.grad_ref, f32[4,2,1024]{2,1,0:T(2,128)} %constant_dynamic-update-slice_fusion.lse_ref, f32[4,2,1024]{2,1,0:T(2,128)} %bitcast.233), custom_call_target="tpu_custom_call" | custom-call | flops 10737418240 | bytes 3145728 | tf_op jit(solution)/shard_map/attend_back/pallas_call | solution.py:186
  305.0 16.0 %collective-permute-done.39 = bf16[64,2048]{1,0:T(8,128)(2,1)} collective-permute-done((bf16[64,2048]{1,0:T(8,128)(2,1)}, bf16[64,2048]{1,0:T(8,128)(2,1)}, u32[]{:S(2)}, u32[]{:S(2)}) %collective-permute-start.39) | collective-permute-done | bytes 262176 | tf_op jit(solution)/shard_map/ppermute | solution.py:260
  323.2 13.8 %attend_back.3 = bf16[1024,768]{1,0:T(8,128)(2,1)} custom-call(bf16[1024,1536]{1,0:T(8,128)(2,1)} %convolution_convert_fusion.query_ref.all_ref, bf16[1024,512]{1,0:T(8,128)(2,1)} %pad_maximum_fusion.6.grad_ref, f32[4,2,1024]{2,1,0:T(2,128)} %constant_dynamic-update-slice_fusion.lse_ref, f32[4,2,1024]{2,1,0:T(2,128)} %bitcast.234), custom_call_target="tpu_custom_call" | custom-call | flops 10737418240 | bytes 3145728 | tf_op jit(solution)/shard_map/attend_back/pallas_call | solution.py:186
  347.4 4.9 %collective-permute-done.36 = bf16[64,1024]{1,0:T(8,128)(2,1)S(1)} collective-permute-done((bf16[64,1024]{1,0:T(8,128)(2,1)S(1)}, bf16[64,1024]{1,0:T(8,128)(2,1)S(1)}, u32[]{:S(2)}, u32[]{:S(2)}) %collective-permute-start.36) | collective-permute-done | bytes 131104 | tf_op jit(solution)/shard_map/ppermute | solution.py:260
  353.6 11.0 %collective-permute-done.35 = bf16[64,1024]{1,0:T(8,128)(2,1)S(1)} collective-permute-done((bf16[64,1024]{1,0:T(8,128)(2,1)S(1)}, bf16[64,1024]{1,0:T(8,128)(2,1)S(1)}, u32[]{:S(2)}, u32[]{:S(2)}) %collective-permute-start.35) | collective-permute-done | bytes 131104 | tf_op jit(solution)/shard_map/ppermute | solution.py:260
  376.1 10.7 %collective-permute-done.27 = bf16[64,768]{1,0:T(8,128)(2,1)S(1)} collective-permute-done((bf16[64,768]{1,0:T(8,128)(2,1)S(1)}, bf16[64,768]{1,0:T(8,128)(2,1)S(1)}, u32[]{:S(2)}, u32[]{:S(2)}) %collective-permute-start.27) | collective-permute-done | bytes 98336 | tf_op jit(solution)/shard_map/ppermute | solution.py:260
  388.7 4.8 %multiply_reduce_fusion = (f32[1024]{0:T(1024)S(1)}, f32[1024]{0:T(1024)S(1)}, f32[1024,1024]{1,0:T(8,128)}, f32[1024,1024]{1,0:T(8,128)S(1)}) fusion(f32[1024]{0:T(1024)S(1)} %add_rsqrt_fusion, f32[1024]{0:T(1024)S(1)} %broadcast_multiply_fusion, bf16[512,1024]{1,0:T(8,128)(2,1)S(1)} %copy-done.13, bf16[512,1024]{1,0:T(8,128)(2,1)S(1)} %bitcast.191, ...), kind=kOutput, calls=%fused_computation.6 | convolution fusion | flops 1621096448 | bytes 17842176 | tf_op jit(solution)/shard_map/dot_general | solution.py:26
  397.2 21.3 %collective-permute-done.24 = f32[1,6144]{1,0:T(1,128)S(1)} collective-permute-done((f32[1,6144]{1,0:T(1,128)S(1)}, f32[1,6144]{1,0:T(1,128)S(1)}, u32[]{:S(2)}, u32[]{:S(2)}) %collective-permute-start.24) | collective-permute-done | bytes 24608 | tf_op jit(solution)/shard_map/ppermute | solution.py:220
  419.9 5.7 %all-to-all-start.2 = ((bf16[16,2,192]{2,1,0:T(2,128)(2,1)}), bf16[16,2,192]{2,1,0:T(2,128)(2,1)S(1)}, u32[]{:S(2)}, u32[]{:S(2)}) async-start(bf16[16,2,192]{2,1,0:T(2,128)(2,1)} %reshape.186), calls=%async_computation.2 | async-start | bytes 32768 | tf_op jit(solution)/shard_map/all_to_all | solution.py:482
  439.5 4.4 all-to-all-done.3
  450.4 5.9 %collective-permute-done.31 = bf16[64,768]{1,0:T(8,128)(2,1)S(1)} collective-permute-done((bf16[64,768]{1,0:T(8,128)(2,1)S(1)}, bf16[64,768]{1,0:T(8,128)(2,1)S(1)}, u32[]{:S(2)}, u32[]{:S(2)}) %collective-permute-start.31) | collective-permute-done | bytes 98336 | tf_op jit(solution)/shard_map/ppermute | solution.py:260
  (283 shorter events, 173.3 us)
Async XLA Ops:
  7.2 100.3 %all-gather.3.cloned.1.call-start = ((), (), s32[]{:S(2)}) async-start(), calls=%async_computation.5 | async-start | bytes 3342336 | tf_op jit(solution)/shard_map/all_gather | solution.py:339
  25.4 57.0 %collective-permute-start.3 = (bf16[64,2048]{1,0:T(8,128)(2,1)}, bf16[64,2048]{1,0:T(8,128)(2,1)S(1)}, u32[]{:S(2)}, u32[]{:S(2)}) collective-permute-start(bf16[64,2048]{1,0:T(8,128)(2,1)} %param.14), channel_id=1, source_target_pairs={{0,8},{2,10},{4,12},{6,14},{8,16},{10,18},{12,20},{14,22},{16,24},... | collective-permute-start | bytes 786440 | tf_op jit(solution)/shard_map/ppermute | solution.py:260
  26.0 56.4 %collective-permute-start.4 = (bf16[64,2048]{1,0:T(8,128)(2,1)}, bf16[64,2048]{1,0:T(8,128)(2,1)S(1)}, u32[]{:S(2)}, u32[]{:S(2)}) collective-permute-start(bf16[64,2048]{1,0:T(8,128)(2,1)} %param.14), channel_id=1, source_target_pairs={{0,16},{2,18},{4,20},{6,22},{8,24},{10,26},{12,28},{14,30},{16,0},... | collective-permute-start | bytes 786440 | tf_op jit(solution)/shard_map/ppermute | solution.py:260
  29.5 54.4 %collective-permute-start.5 = (bf16[64,2048]{1,0:T(8,128)(2,1)}, bf16[64,2048]{1,0:T(8,128)(2,1)}, u32[]{:S(2)}, u32[]{:S(2)}) collective-permute-start(bf16[64,2048]{1,0:T(8,128)(2,1)} %param.14), channel_id=1, source_target_pairs={{0,24},{2,26},{4,28},{6,30},{8,0},{10,2},{12,4},{14,6},{16,8},{18,... | collective-permute-start | bytes 786440 | tf_op jit(solution)/shard_map/ppermute | solution.py:260
  30.2 50.2 %collective-permute-start.1 = (bf16[64,1024]{1,0:T(8,128)(2,1)}, bf16[64,1024]{1,0:T(8,128)(2,1)}, u32[]{:S(2)}, u32[]{:S(2)}) collective-permute-start(bf16[64,1024]{1,0:T(8,128)(2,1)} %param.13), channel_id=1, source_target_pairs={{0,16},{2,18},{4,20},{6,22},{8,24},{10,26},{12,28},{14,30},{16,0},... | collective-permute-start | bytes 393224 | tf_op jit(solution)/shard_map/ppermute | solution.py:260
  36.1 45.8 %collective-permute-start.2 = (bf16[64,1024]{1,0:T(8,128)(2,1)}, bf16[64,1024]{1,0:T(8,128)(2,1)}, u32[]{:S(2)}, u32[]{:S(2)}) collective-permute-start(bf16[64,1024]{1,0:T(8,128)(2,1)} %param.13), channel_id=1, source_target_pairs={{0,24},{2,26},{4,28},{6,30},{8,0},{10,2},{12,4},{14,6},{16,8},{18,... | collective-permute-start | bytes 393224 | tf_op jit(solution)/shard_map/ppermute | solution.py:260
  37.7 42.5 %all-to-all-start.1 = ((bf16[16,2,192]{2,1,0:T(2,128)(2,1)}), bf16[16,2,192]{2,1,0:T(2,128)(2,1)S(1)}, u32[]{:S(2)}, u32[]{:S(2)}) async-start(bf16[16,2,192]{2,1,0:T(2,128)(2,1)} %reshape.184), calls=%async_computation.1 | async-start | bytes 32768 | tf_op jit(solution)/shard_map/all_to_all | solution.py:329
  41.2 123.4 %all-gather.5.cloned.1.call-start = ((), (), s32[]{:S(2)}) async-start(), calls=%async_computation.6 | async-start | bytes 4456448 | tf_op jit(solution)/shard_map/all_gather | solution.py:340
  42.0 427.8 %reduce-scatter.2.cloned.1.call-start = ((), (), s32[]{:S(2)}) async-start(), calls=%async_computation.7 | async-start | bytes 4456448 | tf_op jit(solution)/shard_map/reduce_scatter | solution.py:395
  80.4 26.1 %collective-permute-start.6 = (bf16[512,1024]{1,0:T(8,128)(2,1)S(1)}, bf16[512,1024]{1,0:T(8,128)(2,1)S(1)}, u32[]{:S(2)}, u32[]{:S(2)}) collective-permute-start(bf16[512,1024]{1,0:T(8,128)(2,1)S(1)} %bitcast.185), channel_id=1, source_target_pairs={{1,0},{0,1},{3,2},{2,3},{5,4},{4,5},{7,6},{6,7},{9,8},{8,9},{11,10... | collective-permute-start | bytes 3145736 | tf_op jit(solution)/shard_map/ppermute | solution.py:220
  81.9 49.7 %collective-permute-start.11 = (bf16[512,1024]{1,0:T(8,128)(2,1)S(1)}, bf16[512,1024]{1,0:T(8,128)(2,1)}, u32[]{:S(2)}, u32[]{:S(2)}) collective-permute-start(bf16[512,1024]{1,0:T(8,128)(2,1)S(1)} %bitcast.183), channel_id=1, source_target_pairs={{1,0},{0,1},{3,2},{2,3},{5,4},{4,5},{7,6},{6,7},{9,8},{8,9},{11,10... | collective-permute-start | bytes 3145736 | tf_op jit(solution)/shard_map/ppermute | solution.py:220
  87.7 42.6 %collective-permute-start.7 = (bf16[4,64,1024]{2,1,0:T(8,128)(2,1)S(1)}, bf16[4,64,1024]{2,1,0:T(8,128)(2,1)}, u32[]{:S(2)}, u32[]{:S(2)}) collective-permute-start(bf16[4,64,1024]{2,1,0:T(8,128)(2,1)S(1)} %bitcast_dynamic-update-slice_fusion.4), channel_id=1, source_target_pairs={{0,4},{2,6},{4,0},{6,2},{8,12},{10,14},{12,8},{14,10},{16,20},{18,... | collective-permute-start | bytes 1572872 | tf_op jit(solution)/shard_map/ppermute | solution.py:257
  94.8 56.3 %collective-permute-start.10 = (bf16[4,64,2048]{2,1,0:T(8,128)(2,1)}, bf16[4,64,2048]{2,1,0:T(8,128)(2,1)}, u32[]{:S(2)}, u32[]{:S(2)}) collective-permute-start(bf16[4,64,2048]{2,1,0:T(8,128)(2,1)} %bitcast_dynamic-update-slice_fusion), channel_id=1, source_target_pairs={{0,4},{2,6},{4,0},{6,2},{8,12},{10,14},{12,8},{14,10},{16,20},{18,... | collective-permute-start | bytes 3145736 | tf_op jit(solution)/shard_map/ppermute | solution.py:257
  161.4 25.7 %collective-permute-start.13 = (bf16[512,1024]{1,0:T(8,128)(2,1)}, bf16[512,1024]{1,0:T(8,128)(2,1)}, u32[]{:S(2)}, u32[]{:S(2)}) collective-permute-start(bf16[512,1024]{1,0:T(8,128)(2,1)} %add_convert_fusion.5.hidden_ref), channel_id=1, source_target_pairs={{1,0},{0,1},{3,2},{2,3},{5,4},{4,5},{7,6},{6,7},{9,8},{8,9},{11,10... | collective-permute-start | bytes 3145736 | tf_op jit(solution)/shard_map/ppermute | solution.py:220
  212.3 25.9 %collective-permute-start.15 = (bf16[8,64,2048]{2,1,0:T(8,128)(2,1)}, bf16[8,64,2048]{2,1,0:T(8,128)(2,1)}, u32[]{:S(2)}, u32[]{:S(2)}) collective-permute-start(bf16[8,64,2048]{2,1,0:T(8,128)(2,1)} %get-tuple-element.135), channel_id=1, source_target_pairs={{0,2},{2,0},{4,6},{6,4},{8,10},{10,8},{12,14},{14,12},{16,18},{18,... | collective-permute-start | bytes 6291464 | tf_op jit(solution)/shard_map/ppermute | solution.py:254
  212.3 25.9 %collective-permute-start.14 = (bf16[512,1024]{1,0:T(8,128)(2,1)}, bf16[512,1024]{1,0:T(8,128)(2,1)}, u32[]{:S(2)}, u32[]{:S(2)}) collective-permute-start(bf16[512,1024]{1,0:T(8,128)(2,1)} %get-tuple-element.93), channel_id=1, source_target_pairs={{0,1},{1,0},{2,3},{3,2},{4,5},{5,4},{6,7},{7,6},{8,9},{9,8},{10,11... | collective-permute-start | bytes 3145736 | tf_op jit(solution)/shard_map/ppermute | solution.py:223
  242.7 25.6 %collective-permute-start.17 = (bf16[4,64,2048]{2,1,0:T(8,128)(2,1)}, bf16[4,64,2048]{2,1,0:T(8,128)(2,1)}, u32[]{:S(2)}, u32[]{:S(2)}) collective-permute-start(bf16[4,64,2048]{2,1,0:T(8,128)(2,1)} %get-tuple-element.144), channel_id=1, source_target_pairs={{0,4},{2,6},{4,0},{6,2},{8,12},{10,14},{12,8},{14,10},{16,20},{18,... | collective-permute-start | bytes 3145736 | tf_op jit(solution)/shard_map/ppermute | solution.py:257
  292.8 30.3 %collective-permute-start.20 = (bf16[8,64,768]{2,1,0:T(8,128)(2,1)}, bf16[8,64,768]{2,1,0:T(8,128)(2,1)}, u32[]{:S(2)}, u32[]{:S(2)}) collective-permute-start(bf16[8,64,768]{2,1,0:T(8,128)(2,1)} %get-tuple-element.152), channel_id=1, source_target_pairs={{0,2},{2,0},{4,6},{6,4},{8,10},{10,8},{12,14},{14,12},{16,18},{18,... | collective-permute-start | bytes 2359304 | tf_op jit(solution)/shard_map/ppermute | solution.py:254
  295.8 25.2 %collective-permute-start.39 = (bf16[64,2048]{1,0:T(8,128)(2,1)}, bf16[64,2048]{1,0:T(8,128)(2,1)}, u32[]{:S(2)}, u32[]{:S(2)}) collective-permute-start(bf16[64,2048]{1,0:T(8,128)(2,1)} %get-tuple-element.156), channel_id=1, source_target_pairs={{0,16},{2,18},{4,20},{6,22},{8,24},{10,26},{12,28},{14,30},{16,0},... | collective-permute-start | bytes 786440 | tf_op jit(solution)/shard_map/ppermute | solution.py:260
  297.4 23.6 %collective-permute-start.38 = (bf16[64,2048]{1,0:T(8,128)(2,1)}, bf16[64,2048]{1,0:T(8,128)(2,1)}, u32[]{:S(2)}, u32[]{:S(2)}) collective-permute-start(bf16[64,2048]{1,0:T(8,128)(2,1)} %get-tuple-element.154), channel_id=1, source_target_pairs={{0,8},{2,10},{4,12},{6,14},{8,16},{10,18},{12,20},{14,22},{16,24},... | collective-permute-start | bytes 786440 | tf_op jit(solution)/shard_map/ppermute | solution.py:260
  300.3 22.8 %collective-permute-start.21 = (bf16[4,64,1024]{2,1,0:T(8,128)(2,1)}, bf16[4,64,1024]{2,1,0:T(8,128)(2,1)}, u32[]{:S(2)}, u32[]{:S(2)}) collective-permute-start(bf16[4,64,1024]{2,1,0:T(8,128)(2,1)} %get-tuple-element.157), channel_id=1, source_target_pairs={{0,4},{2,6},{4,0},{6,2},{8,12},{10,14},{12,8},{14,10},{16,20},{18,... | collective-permute-start | bytes 1572872 | tf_op jit(solution)/shard_map/ppermute | solution.py:257
  304.4 61.1 %collective-permute-start.19 = (bf16[512,1024]{1,0:T(8,128)(2,1)}, bf16[512,1024]{1,0:T(8,128)(2,1)}, u32[]{:S(2)}, u32[]{:S(2)}) collective-permute-start(bf16[512,1024]{1,0:T(8,128)(2,1)} %get-tuple-element.104), channel_id=1, source_target_pairs={{0,1},{1,0},{2,3},{3,2},{4,5},{5,4},{6,7},{7,6},{8,9},{9,8},{10,11... | collective-permute-start | bytes 3145736 | tf_op jit(solution)/shard_map/ppermute | solution.py:223
  340.6 46.2 %collective-permute-start.22 = (bf16[8,64,768]{2,1,0:T(8,128)(2,1)S(1)}, bf16[8,64,768]{2,1,0:T(8,128)(2,1)S(1)}, u32[]{:S(2)}, u32[]{:S(2)}) collective-permute-start(bf16[8,64,768]{2,1,0:T(8,128)(2,1)S(1)} %get-tuple-element.150), channel_id=1, source_target_pairs={{0,2},{2,0},{4,6},{6,4},{8,10},{10,8},{12,14},{14,12},{16,18},{18,... | collective-permute-start | bytes 2359304 | tf_op jit(solution)/shard_map/ppermute | solution.py:254
  394.8 68.7 %collective-permute-start.23 = (bf16[512,1024]{1,0:T(8,128)(2,1)}, bf16[512,1024]{1,0:T(8,128)(2,1)}, u32[]{:S(2)}, u32[]{:S(2)}) collective-permute-start(bf16[512,1024]{1,0:T(8,128)(2,1)} %slice.73), channel_id=1, source_target_pairs={{0,1},{1,0},{2,3},{3,2},{4,5},{5,4},{6,7},{7,6},{8,9},{9,8},{10,11... | collective-permute-start | bytes 3145736 | tf_op jit(solution)/shard_map/ppermute | solution.py:223
  (65 other events, 1101.5 us)
Sparse Core Ops, SparseCore 0:
  10.9 67.3 all-gather.2
  80.4 63.2 all-gather.4
  301.6 86.9 reduce-scatter.1

commit v3 on v2

--- a/solution.py
+++ b/solution.py
@@ -323,46 +323,66 @@
         concat_axis=0,
         tiled=True,
     )
-    cond_all, out_shard, up_shard = after((cond_all, w_out, w_up))
-    out_pieces, up_pieces = gather_z(out_shard), gather_z(up_shard)
     mod_cols = (mm(cond_all, w_ada) + b_ada.astype(wide)).astype(low)
+    peer_latents = [fetch(own_latents, step) for step in range(1, splits)]
+    mod_cols, peer_latents = after((mod_cols, peer_latents))
     modulation = lax.all_to_all(
         mod_cols, "fsdp", split_axis=0, concat_axis=1, tiled=True
     ).astype(wide)
-    modulation, out_pieces, up_pieces = after((modulation, out_pieces, up_pieces))
-    out_pair, up_pair = gather_x(out_pieces), gather_x(up_pieces)
+    modulation, out_shard = after((modulation, w_out))
+    out_pieces = gather_z(out_shard)
     shift_one, scale_one, gate_one, shift_two, scale_two, gate_two = [
         modulation[:, position * width : (position + 1) * width] for position in range(6)
     ]
     columns = heads * 3 * HD
     qkv_shard = lax.dynamic_slice_in_dim(w_qkv, me * columns, columns, 1)
     qkv_half = lax.all_gather(qkv_shard, "fsdp", axis=0, tiled=True)
-    down_full = lax.all_gather(w_down.T, "fsdp", axis=0, tiled=True)
-
-    latents_all = jnp.concatenate(everyone(own_latents), 0)
+    up_down = lax.all_gather(jnp.concatenate([w_up, w_down.T], 1), "fsdp", axis=0, tiled=True)
+    units = w_up.shape[1]
+
+    latents_all = jnp.concatenate([own_latents] + peer_latents, 0)
     cotangent_all = jnp.concatenate(everyone(own_cotangent), 0)
     grad_rows = (gate_two * cotangent_all.astype(wide)).astype(low)
 
     normed_all, inverse_all = normalize(latents_all.astype(wide))
     hidden_one = (normed_all * (1.0 + scale_one) + shift_one).astype(low)
     qkv = mm(hidden_one, qkv_half).astype(low)
+    qkv, out_pieces = after((qkv, out_pieces))
+    out_pair = gather_x(out_pieces)
     attn_peers, lse_peers = attend(qkv, tokens, 1, splits - 1)
-    attn_peers, out_pair = after((attn_peers, out_pair))
+    attn_peers, qkv, out_pair = after((attn_peers, qkv, out_pair))
     out_pair = gather_core(out_pair)
-    peer_rows = [attn_peers[r * tokens : (r + 1) * tokens] for r in range(splits - 1)]
-    arrived = [send(value, r + 1) for r, value in enumerate(peer_rows)]
+    blocks = [None] + [attn_peers[r * tokens : (r + 1) * tokens] for r in range(splits - 1)]
+    theirs = [{} for _ in range(splits)]
+    for r in range(1, splits):
+        for q in range(1, splits):
+            theirs[(r + q) % splits][q] = fetch(blocks[r], q)
     attn_own, lse_own = attend(qkv, tokens, 0, 1)
-    attn_own, out_pair, up_pair = after((attn_own, out_pair, up_pair))
-    out_full, up_pair = gather_end(out_pair), gather_core(up_pair)
-    attn_rows = in_order([attn_own] + arrived[::-1], 1)
-    branch_one = mm(attn_rows, out_full)
-    inputs = own_latents.astype(wide)
-    middle = inputs + gate_one * branch_one
-    normed_two, inverse_two = normalize(middle)
-    hidden_two = (normed_two * (1.0 + scale_two) + shift_two).astype(low)
-
-    hidden_pieces = everyone(hidden_two)
-    up_full = gather_end(up_pair)
+    blocks[0] = attn_own
+    attn_own, out_pair, theirs = after((attn_own, out_pair, theirs))
+    for q in range(1, splits):
+        theirs[q][q] = fetch(attn_own, q)
+    out_full = gather_end(out_pair)
+
+    def to_feed(rows, heads_of, piece):
+        inputs = latents_all[piece * tokens : (piece + 1) * tokens].astype(wide)
+        attn_rows = in_order([rows] + [heads_of[q] for q in range(1, splits)], 1)
+        branch_one = mm(attn_rows, out_full)
+        middle = inputs + gate_one * branch_one
+        normed, inverse = normalize(middle)
+        hidden = (normed * (1.0 + scale_two) + shift_two).astype(low)
+        return hidden, attn_rows, branch_one, middle, normed, inverse
+
+    own_theirs = theirs[0]
+    hidden_two, attn_rows, branch_one, middle, normed_two, inverse_two = to_feed(
+        attn_own, own_theirs, 0
+    )
+    hidden_two, theirs = after((hidden_two, theirs))
+    hidden_pieces = [hidden_two] + [
+        to_feed(blocks[r], theirs[r], r)[0] for r in range(1, splits)
+    ]
+
+    up_full, down_full = up_down[:, :units], up_down[:, units:]
     buffers, grad_parts, branch_parts = None, [], []
     for piece in range(splits):
         act, grad_up, branch_part, grad_part = feed(
@@ -377,8 +397,6 @@
         buffers = (act, grad_up)
         grad_parts.append(grad_part)
         branch_parts.append(branch_part)
-        if piece + 1 < splits:
-            hidden_pieces[piece + 1], buffers = after((hidden_pieces[piece + 1], buffers))
 
     def send_parts(parts):
         return [send(parts[step].astype(low), step) for step in range(1, splits)]
@@ -389,9 +407,9 @@
         return own
 
     grad_sent = send_parts(grad_parts)
+    term_down = mm(grad_rows, act, TN).astype(low)
     term_up = mm(jnp.concatenate(hidden_pieces, 0), grad_up, TN).astype(low)
     up_pair = scatter_core(term_up)
-    term_down = mm(grad_rows, act, TN).astype(low)
     grad_w_down = lax.psum_scatter(term_down, "fsdp", scatter_dimension=0, tiled=True)
     grad_sent, up_pair, term_down, branch_parts = after(
         (grad_sent, up_pair, term_down, branch_parts)
@@ -416,11 +434,9 @@
     grad_arrived = [send(grad_pieces[r], r) for r in range(1, splits)]
     term_out = mm(attn_rows, grad_branch_one, TN).astype(low)
     out_pair = scatter_core(term_out)
-    grad_arrived, branch_parts, up_pair, out_pair = after(
-        (grad_arrived, branch_parts, up_pair, out_pair)
-    )
+    grad_arrived, branch_parts, out_pair = after((grad_arrived, branch_parts, out_pair))
     branch_sent = send_parts(branch_parts)
-    up_pieces, out_pair = scatter_z(up_pair), scatter_x(out_pair)
+    out_pair = scatter_x(out_pair)
     grad_heads = jnp.concatenate([grad_pieces[0]] + grad_arrived[::-1], 0)
     attn_all = jnp.concatenate([attn_own, attn_peers], 0)
     lse = jnp.concatenate([lse_own, lse_peers], 2)
@@ -430,64 +446,65 @@
     pairs = heads // 2
     groups = 2 if pairs % 2 == 0 else 1
     each = pairs // groups
-    grad_qkv, qkv_pairs = [], []
+    size = each * 6 * HD
+    qkv_pieces, hidden_grads = [], []
     for group in range(groups):
-        grad_qkv.append(attend_back(qkv, grad_heads, lse, delta, group * each, each))
-        term_qkv = mm(hidden_one, grad_qkv[-1], TN).astype(low)
-        pair = scatter_core(term_qkv)
-        if group + 1 < groups:
-            pair, grad_heads, out_pair = after((pair, grad_heads, out_pair))
-            out_pieces = scatter_z(out_pair)
-            pair = scatter_x(pair)
+        if group:
+            qkv_pair, grad_heads = after((qkv_pair, grad_heads))
+            qkv_pair = scatter_x(qkv_pair)
+        value = attend_back(qkv, grad_heads, lse, delta, group * each, each)
+        if group == 0:
+            value, up_pair, out_pair = after((value, up_pair, out_pair))
+            up_pieces, out_pieces = scatter_z(up_pair), scatter_z(out_pair)
         else:
-            pair, grad_qkv = after((pair, grad_qkv))
-        qkv_pairs.append(pair)
-    if groups == 1:
-        out_pieces = scatter_z(out_pair)
-    size = each * 6 * HD
-    hidden_grad_all = sum(
-        mm(value, qkv_half[:, group * size : (group + 1) * size], NT)
-        for group, value in enumerate(grad_qkv)
-    )
+            value, qkv_pair, up_pieces, out_pieces, branch_sent = after(
+                (value, qkv_pair, up_pieces, out_pieces, branch_sent)
+            )
+            qkv_pieces = scatter_z(qkv_pair)
+        term_qkv = mm(hidden_one, value, TN).astype(low)
+        qkv_pair = scatter_core(term_qkv)
+        term_qkv, value = after((term_qkv, value))
+        hidden_grads.append((value, qkv_half[:, group * size : (group + 1) * size]))
+    hidden_grad_all = sum(mm(value, weight, NT) for value, weight in hidden_grads)
     grad_shift_one = jnp.sum(hidden_grad_all, 0)
     grad_scale_one = jnp.sum(hidden_grad_all * normed_all, 0)
+    branch_two = add_parts(branch_parts[0], branch_sent)
+    grad_gate_two = jnp.sum(grad_mixed * branch_two, 0)
+
+    grad_mod_part = jnp.concatenate(
+        [
+            grad_shift_one,
+            grad_scale_one,
+            grad_gate_one,
+            grad_shift_two,
+            grad_scale_two,
+            grad_gate_two,
+        ]
+    )[None]
+    grad_mod = seq_sum(grad_mod_part).astype(low)
     hidden_parts = [hidden_grad_all[r * tokens : (r + 1) * tokens] for r in range(splits)]
+    qkv_pair, grad_mod, hidden_parts = after((qkv_pair, grad_mod, hidden_parts))
     hidden_sent = send_parts(hidden_parts)
-    qkv_pairs[-1] = scatter_x(qkv_pairs[-1])
+    qkv_pair = scatter_x(qkv_pair)
+    grad_w_out = seq_sum(scatter_end(out_pieces).astype(low))
     grad_w_up = scatter_end(up_pieces)
-    grad_w_out = scatter_end(out_pieces).astype(low)
-    grad_w_qkv = jnp.concatenate(
-        [scatter_end(scatter_z(pair)).astype(low) for pair in qkv_pairs], 1
-    )
-    branch_two = add_parts(branch_parts[0], branch_sent)
     mixed = (middle + gate_two * branch_two).astype(low)
-    grad_gate_two = jnp.sum(grad_mixed * branch_two, 0)
-    grad_hidden_one = add_parts(hidden_parts[0], hidden_sent)
-    grad_latents = grad_middle + norm_grad(
-        normed_all[:tokens], inverse_all[:tokens], grad_hidden_one * (1.0 + scale_one)
-    )
-
-    grad_mod = seq_sum(
-        jnp.concatenate(
-            [
-                grad_shift_one,
-                grad_scale_one,
-                grad_gate_one,
-                grad_shift_two,
-                grad_scale_two,
-                grad_gate_two,
-            ]
-        )[None]
-    ).astype(low)
     grad_mod_cols = lax.all_to_all(grad_mod, "fsdp", split_axis=1, concat_axis=0, tiled=True)
     grad_w_ada = mm(cond_all, grad_mod_cols, TN)
     grad_b_ada = jnp.sum(grad_mod_cols.astype(wide), 0)
     cond_term = mm(grad_mod_cols, w_ada, NT).astype(low)
+    cond_term, qkv_pair, qkv_pieces, mixed = after((cond_term, qkv_pair, qkv_pieces, mixed))
+    shards_qkv = [scatter_end(qkv_pieces).astype(low)] if groups == 2 else []
+    qkv_pieces = scatter_z(qkv_pair)
     cond_terms = lax.all_to_all(cond_term, "fsdp", split_axis=0, concat_axis=0, tiled=True)
     grad_cond = silu_back(jnp.sum(cond_terms.astype(wide), 0, keepdims=True))[0]
-
-    grad_w_qkv = in_order(everyone(grad_w_qkv), 1).astype(wide)
-    grad_w_out = seq_sum(grad_w_out)
+    grad_hidden_one = add_parts(hidden_parts[0], hidden_sent)
+    grad_latents = grad_middle + norm_grad(
+        normed_all[:tokens], inverse_all[:tokens], grad_hidden_one * (1.0 + scale_one)
+    )
+    qkv_pieces, grad_latents, grad_cond = after((qkv_pieces, grad_latents, grad_cond))
+    shards_qkv.append(scatter_end(qkv_pieces).astype(low))
+    grad_w_qkv = in_order(everyone(jnp.concatenate(shards_qkv, 1)), 1).astype(wide)
     return (
         mixed[None],
         grad_latents[None],

time: 485 us -> 431 us (0.89)
  waiting for transfers between devices: 174 us -> 108 us
  starting transfers between devices: 48.3 us -> 73.2 us
  blocking collectives: 13.8 us -> 0 us
    ppermute x18 -> x15, waiting for transfers between devices: 61.7 us -> 2.31 us  [z_send(): lax.ppermute(value, 'fsdp', [(i, (i + 4 * step) % shards) for i in range(...]
    all_to_all x1, waiting for transfers between devices: 38.1 us -> 5.58 us  [per_device(): lax.all_to_all(mod_cols, 'fsdp', split_axis=0, concat_axis=1, tiled=True)]
    ppermute x6 -> x5, waiting for transfers between devices: 0.02 us -> 23.2 us  [x_swap(): return lax.ppermute(value, 'fsdp', [(i, i ^ 2) for i in range(shards)])]
    ppermute x6 -> x7, waiting for transfers between devices: 41.8 us -> 26 us  [fetch(): lax.ppermute(value, 'seq', [((i + step) % splits, i) for i in range(split...]
    ppermute x18 -> x15, starting transfers between devices: 17.8 us -> 32.6 us  [z_send(): lax.ppermute(value, 'fsdp', [(i, (i + 4 * step) % shards) for i in range(...]
    all_to_all x1 -> x0, blocking collectives: 13.8 us -> none  [per_device(): lax.all_to_all(jnp.broadcast_to(cond_act.astype(low), (shards, width)), '...]
    all_gather x1, waiting for transfers between devices: 0.02 us -> 12.4 us  [per_device(): qkv_half = lax.all_gather(qkv_shard, 'fsdp', axis=0, tiled=True)]
    dynamic_update_slice x8 -> x4, local copies, waits for them, and re-layouts: 8.52 us -> 0.06 us  [gather_x(): lax.dynamic_update_slice_in_dim(line, piece[None], (z_at - step) % depth, 0)]
  transfers between devices with their start and end apart: 47 -> 43, of which waited for: 18 -> 18; matrix products, arithmetic and copies ran while one was open for 22% -> 27% of each run, Pallas kernels for 12% -> 13%
where the time goes in v3:
time: 431 us; the launch traced here: 425 us
  waiting for transfers between devices  108 us (25%)
  Pallas kernels  88.9 us (21%)
  starting transfers between devices  73.2 us (17%)
  other arithmetic  52.9 us (12%)
  matrix products  48.9 us (11%)
  local copies, waits for them, and re-layouts  38.8 us (9%)
  between operations  15.2 us (4%)
    dot_general x14, matrix products, mm(): return lax.dot_general(a, b, dims, preferred_element_type=jnp.float32)  48.9 us
    ppermute x15, starting transfers between devices, z_send(): lax.ppermute(value, 'fsdp', [(i, (i + 4 * step) % shards) for i in range(...  32.6 us
    pallas_call x2, Pallas kernels, feed(): pl.pallas_call(partial(feed_kernel, int(aliased)), grid=(units // block,)...  32.1 us
    pallas_call x2, Pallas kernels, attend(): pl.pallas_call(attend_kernel, grid=(pairs, count), in_specs=[pl.BlockSpec...  29.2 us
    pallas_call x2, Pallas kernels, attend_back(): pl.pallas_call(attend_back_kernel, grid=(pairs,), in_specs=[pl.BlockSpec(...  27.5 us
    ppermute x7, waiting for transfers between devices, fetch(): lax.ppermute(value, 'seq', [((i + step) % splits, i) for i in range(split...  26 us
    ppermute x5, waiting for transfers between devices, x_swap(): return lax.ppermute(value, 'fsdp', [(i, i ^ 2) for i in range(shards)])  23.2 us
    ppermute x4, waiting for transfers between devices, send(): lax.ppermute(value, 'seq', [(i, (i + step) % splits) for i in range(split...  16.4 us
  transfers between devices with their start and end apart: 43, of which 18 were waited for; matrix products, arithmetic and copies ran while one was open for 27% of the time, Pallas kernels for 13%

profile of v3, /device:TPU:0, one launch (start us, length us, event | category | flops | bytes accessed | tf_op | source)
XLA Modules:
  0.0 425.5 jit_solution(696388998261186072)
XLA Ops:
  16.7 5.9 %all-to-all-start = ((bf16[16,2,512]{2,1,0:T(2,128)(2,1)}), bf16[16,2,512]{2,1,0:T(2,128)(2,1)S(1)}, u32[]{:S(2)}, u32[]{:S(2)}) async-start(bf16[16,2,512]{2,1,0:T(2,128)(2,1)} %reshape.168), calls=%async_computation | async-start | bytes 65536 | tf_op jit(solution)/shard_map/all_to_all | solution.py:319
  22.7 6.9 %all-to-all-done = bf16[16,2,512]{2,1,0:T(2,128)(2,1)S(1)} async-done(((bf16[16,2,512]{2,1,0:T(2,128)(2,1)}), bf16[16,2,512]{2,1,0:T(2,128)(2,1)S(1)}, u32[]{:S(2)}, u32[]{:S(2)}) %all-to-all-start) | async-done | bytes 32800 | tf_op jit(solution)/shard_map/all_to_all | solution.py:319
  29.9 7.3 %collective-permute-done = bf16[512,1024]{1,0:T(8,128)(2,1)S(1)} collective-permute-done((bf16[512,1024]{1,0:T(8,128)(2,1)S(1)}, bf16[512,1024]{1,0:T(8,128)(2,1)S(1)}, u32[]{:S(2)}, u32[]{:S(2)}) %collective-permute-start) | collective-permute-done | bytes 1048608 | tf_op jit(solution)/shard_map/ppermute | solution.py:220
  38.5 6.1 %all-to-all-start.1 = ((bf16[16,2,192]{2,1,0:T(2,128)(2,1)}), bf16[16,2,192]{2,1,0:T(2,128)(2,1)S(1)}, u32[]{:S(2)}, u32[]{:S(2)}) async-start(bf16[16,2,192]{2,1,0:T(2,128)(2,1)} %reshape.170), calls=%async_computation.1 | async-start | bytes 32768 | tf_op jit(solution)/shard_map/all_to_all | solution.py:329
  45.8 5.6 %all-to-all-done.1 = bf16[16,2,192]{2,1,0:T(2,128)(2,1)S(1)} async-done(((bf16[16,2,192]{2,1,0:T(2,128)(2,1)}), bf16[16,2,192]{2,1,0:T(2,128)(2,1)S(1)}, u32[]{:S(2)}, u32[]{:S(2)}) %all-to-all-start.1) | async-done | bytes 12320 | tf_op jit(solution)/shard_map/all_to_all | solution.py:329
  55.4 12.4 %all-gather.3.cloned.1.call-done = bf16[1024,1536]{1,0:T(8,128)(2,1)} async-done(((bf16[64,1536]{1,0:T(8,128)(2,1)}), bf16[1024,1536]{1,0:T(8,128)(2,1)}) %all-gather.3.cloned.1.call-update) | async-done | bytes 3145744 | tf_op jit(solution)/shard_map/all_gather | solution.py:339
  67.8 7.6 %convolution_convert_fusion.query_ref.all_ref = bf16[1024,1536]{1,0:T(8,128)(2,1)} fusion(bf16[1024,1536]{1,0:T(8,128)(2,1)} %all-gather.3.cloned.1.call-done, f32[1024]{0:T(1024)S(1)} %bitcast.202, f32[1024]{0:T(1024)S(1)} %bitcast.188, f32[1024]{0:T(1024)S(1)} %add_rsqrt_fusion, f32[1024]{0:T(1024)S(1)} %broadcast_multiply_fusion, ...), kind=kOutput, calls=%fused_computation.9 | convolution fusion | flops 3232235520 | bytes 8404992 | tf_op jit(solution)/shard_map/dot_general | solution.py:26
  77.6 14.7 %attend.2 = (bf16[512,512]{1,0:T(8,128)(2,1)}, f32[4,2,512]{2,1,0:T(2,128)}) custom-call(bf16[1024,1536]{1,0:T(8,128)(2,1)} %convolution_convert_fusion.query_ref.all_ref, bf16[1024,1536]{1,0:T(8,128)(2,1)} %convolution_convert_fusion.query_ref.all_ref), custom_call_target="tpu_custom_call" | custom-call | flops 4294967296 | bytes 3145728 | tf_op jit(solution)/shard_map/attend/pallas_call | solution.py:68
  105.6 14.5 %attend.3 = (bf16[512,512]{1,0:T(8,128)(2,1)}, f32[4,2,512]{2,1,0:T(2,128)}) custom-call(bf16[1024,1536]{1,0:T(8,128)(2,1)} %convolution_convert_fusion.query_ref.all_ref, bf16[1024,1536]{1,0:T(8,128)(2,1)} %convolution_convert_fusion.query_ref.all_ref), custom_call_target="tpu_custom_call" | custom-call | flops 4294967296 | bytes 3145728 | tf_op jit(solution)/shard_map/attend/pallas_call | solution.py:68
  129.1 5.7 %collective-permute-done.7 = bf16[512,512]{1,0:T(8,128)(2,1)S(1)} collective-permute-done((bf16[512,512]{1,0:T(8,128)(2,1)S(1)}, bf16[512,512]{1,0:T(8,128)(2,1)S(1)}, u32[]{:S(2)}, u32[]{:S(2)}) %collective-permute-start.7) | collective-permute-done | bytes 524320 | tf_op jit(solution)/shard_map/ppermute | solution.py:220
  138.0 7.9 %all-gather.5.cloned.1.call-done = bf16[1024,4096]{1,0:T(8,128)(2,1)} async-done(((bf16[64,4096]{1,0:T(8,128)(2,1)}), bf16[1024,4096]{1,0:T(8,128)(2,1)}) %all-gather.5.cloned.1.call-update) | async-done | bytes 8388624 | tf_op jit(solution)/shard_map/all_gather | solution.py:340
  145.9 6.1 %fusion.33 = (bf16[1024,2048]{1,0:T(8,128)(2,1)}, bf16[1024,2048]{1,0:T(8,128)(2,1)}) fusion(bf16[1024,4096]{1,0:T(8,128)(2,1)} %all-gather.5.cloned.1.call-done), kind=kLoop, calls=%fused_computation.166 | loop fusion | bytes 16777216 | tf_op jit(solution)/shard_map/slice | solution.py:385
  152.0 16.4 %feed.2 = (bf16[1024,2048]{1,0:T(8,128)(2,1)}, bf16[1024,2048]{1,0:T(8,128)(2,1)}, f32[512,1024]{1,0:T(8,128)}, f32[512,1024]{1,0:T(8,128)}) custom-call(bf16[512,1024]{1,0:T(8,128)(2,1)} %add_convert_fusion.6.hidden_ref, bf16[1024,1024]{1,0:T(8,128)(2,1)} %multiply_convert_fusion.grad_ref, bf16[1024,2048]{1,0:T(8,128)(2,1)} %get-tuple-element.188.up_ref, ...), custom_call_target="tpu_custom_call" | custom-call | flops 8589934592 | bytes 16777216 | tf_op jit(solution)/shard_map/feed/pallas_call | solution.py:135
  168.5 15.6 %feed.3 = (bf16[1024,2048]{1,0:T(8,128)(2,1)}, bf16[1024,2048]{1,0:T(8,128)(2,1)}, bf16[512,1024]{1,0:T(8,128)(2,1)}, bf16[512,1024]{1,0:T(8,128)(2,1)}) custom-call(bf16[512,1024]{1,0:T(8,128)(2,1)} %add_convert_fusion.5.hidden_ref, bf16[1024,1024]{1,0:T(8,128)(2,1)} %multiply_convert_fusion.grad_ref, ...), custom_call_target="tpu_custom_call", output_to_operand_aliasing={{0}: (4, {}), {1}: (5, {})} | custom-call | flops 8589934592 | bytes 16777216 | tf_op jit(solution)/shard_map/feed/pallas_call | solution.py:135
  184.2 7.4 %convolution_convert_fusion.2 = bf16[1024,2048]{1,0:T(8,128)(2,1)S(1)} fusion(bf16[1024,2048]{1,0:T(8,128)(2,1)} %get-tuple-element.116, bf16[512,1024]{1,0:T(8,128)(2,1)S(1)} %copy-done.27, bf16[512,1024]{1,0:T(8,128)(2,1)S(1)} %copy-done.26), kind=kOutput, calls=%fused_computation.11 | convolution fusion | flops 4301258752 | bytes 10485760 | tf_op jit(solution)/shard_map/dot_general | solution.py:26
  198.8 9.4 %convolution_convert_fusion.1 = bf16[1024,2048]{1,0:T(8,128)(2,1)} fusion(bf16[1024,1024]{1,0:T(8,128)(2,1)} %multiply_convert_fusion.grad_ref, bf16[1024,2048]{1,0:T(8,128)(2,1)} %get-tuple-element.117), kind=kOutput, calls=%fused_computation.10 | convolution fusion | flops 4297064448 | bytes 10485760 | tf_op jit(solution)/shard_map/dot_general | solution.py:26
  208.3 12.6 %collective-permute-done.9 = bf16[512,1024]{1,0:T(8,128)(2,1)} collective-permute-done((bf16[512,1024]{1,0:T(8,128)(2,1)}, bf16[512,1024]{1,0:T(8,128)(2,1)}, u32[]{:S(2)}, u32[]{:S(2)}) %collective-permute-start.9) | collective-permute-done | bytes 1048608 | tf_op jit(solution)/shard_map/ppermute | solution.py:223
  256.4 13.7 %attend_back.2 = bf16[1024,768]{1,0:T(8,128)(2,1)} custom-call(bf16[1024,1536]{1,0:T(8,128)(2,1)} %convolution_convert_fusion.query_ref.all_ref, bf16[1024,512]{1,0:T(8,128)(2,1)} %pad_maximum_fusion.4.grad_ref, f32[4,2,1024]{2,1,0:T(2,128)} %copy-done.64, f32[4,2,1024]{2,1,0:T(2,128)} %bitcast.199), custom_call_target="tpu_custom_call" | custom-call | flops 10737418240 | bytes 3145728 | tf_op jit(solution)/shard_map/attend_back/pallas_call | solution.py:186
  272.3 12.8 %collective-permute-done.14 = bf16[4,64,1024]{2,1,0:T(8,128)(2,1)S(1)} collective-permute-done((bf16[4,64,1024]{2,1,0:T(8,128)(2,1)S(1)}, bf16[4,64,1024]{2,1,0:T(8,128)(2,1)S(1)}, u32[]{:S(2)}, u32[]{:S(2)}) %collective-permute-start.14) | collective-permute-done | bytes 524320 | tf_op jit(solution)/shard_map/ppermute | solution.py:257
  307.3 9.0 %collective-permute-start.18 = (bf16[64,2048]{1,0:T(8,128)(2,1)}, bf16[64,2048]{1,0:T(8,128)(2,1)S(1)}, u32[]{:S(2)}, u32[]{:S(2)}) collective-permute-start(bf16[64,2048]{1,0:T(8,128)(2,1)} %get-tuple-element.205), channel_id=1, source_target_pairs={{0,16},{2,18},{4,20},{6,22},{8,24},{10,26},{12,28},{14,30},{16,0},... | collective-permute-start | bytes 786440 | tf_op jit(solution)/shard_map/ppermute | solution.py:260
  321.2 13.8 %attend_back.3 = bf16[1024,768]{1,0:T(8,128)(2,1)} custom-call(bf16[1024,1536]{1,0:T(8,128)(2,1)} %convolution_convert_fusion.query_ref.all_ref, bf16[1024,512]{1,0:T(8,128)(2,1)} %pad_maximum_fusion.4.grad_ref, f32[4,2,1024]{2,1,0:T(2,128)} %copy-done.64, f32[4,2,1024]{2,1,0:T(2,128)} %bitcast.200), custom_call_target="tpu_custom_call" | custom-call | flops 10737418240 | bytes 3145728 | tf_op jit(solution)/shard_map/attend_back/pallas_call | solution.py:186
  341.3 4.8 %multiply_reduce_fusion = (f32[1024]{0:T(1024)S(1)}, f32[1024]{0:T(1024)S(1)}, f32[1024,1024]{1,0:T(8,128)}, f32[1024,1024]{1,0:T(8,128)S(1)}) fusion(f32[1024]{0:T(1024)S(1)} %add_rsqrt_fusion, f32[1024]{0:T(1024)S(1)} %broadcast_multiply_fusion, bf16[512,1024]{1,0:T(8,128)(2,1)S(1)} %copy-done.10, bf16[512,1024]{1,0:T(8,128)(2,1)S(1)} %bitcast.154, ...), kind=kOutput, calls=%fused_computation.5 | convolution fusion | flops 1621096448 | bytes 17842176 | tf_op jit(solution)/shard_map/dot_general | solution.py:26
  378.6 5.2 %collective-permute-done.26 = bf16[4,64,768]{2,1,0:T(8,128)(2,1)} collective-permute-done((bf16[4,64,768]{2,1,0:T(8,128)(2,1)}, bf16[4,64,768]{2,1,0:T(8,128)(2,1)}, u32[]{:S(2)}, u32[]{:S(2)}) %collective-permute-start.26) | collective-permute-done | bytes 393248 | tf_op jit(solution)/shard_map/ppermute | solution.py:257
  396.8 5.5 %all-to-all-done.3 = bf16[16,2,512]{2,1,0:T(2,128)(2,1)S(1)} async-done(((bf16[16,2,512]{2,1,0:T(2,128)(2,1)}), bf16[16,2,512]{2,1,0:T(2,128)(2,1)S(1)}, u32[]{:S(2)}, u32[]{:S(2)}) %all-to-all-start.3) | async-done | bytes 32800 | tf_op jit(solution)/shard_map/all_to_all | solution.py:499
  (329 shorter events, 183.2 us)
Async XLA Ops:
  7.2 60.6 %all-gather.3.cloned.1.call-start = ((), (), s32[]{:S(2)}) async-start(), calls=%async_computation.5 | async-start | bytes 3342336 | tf_op jit(solution)/shard_map/all_gather | solution.py:339
  9.0 136.9 %all-gather.5.cloned.1.call-start = ((), (), s32[]{:S(2)}) async-start(), calls=%async_computation.6 | async-start | bytes 8912896 | tf_op jit(solution)/shard_map/all_gather | solution.py:340
  11.0 26.2 %collective-permute-start = (bf16[512,1024]{1,0:T(8,128)(2,1)S(1)}, bf16[512,1024]{1,0:T(8,128)(2,1)S(1)}, u32[]{:S(2)}, u32[]{:S(2)}) collective-permute-start(bf16[512,1024]{1,0:T(8,128)(2,1)S(1)} %bitcast.148), channel_id=1, source_target_pairs={{1,0},{0,1},{3,2},{2,3},{5,4},{4,5},{7,6},{6,7},{9,8},{8,9},{11,10... | collective-permute-start | bytes 3145736 | tf_op jit(solution)/shard_map/ppermute | solution.py:220
  44.7 367.1 %reduce-scatter.2.cloned.1.call-start = ((), (), s32[]{:S(2)}) async-start(), calls=%async_computation.7 | async-start | bytes 4456448 | tf_op jit(solution)/shard_map/reduce_scatter | solution.py:413
  51.5 23.9 %collective-permute-start.1 = (bf16[64,1024]{1,0:T(8,128)(2,1)S(1)}, bf16[64,1024]{1,0:T(8,128)(2,1)S(1)}, u32[]{:S(2)}, u32[]{:S(2)}) collective-permute-start(bf16[64,1024]{1,0:T(8,128)(2,1)S(1)} %copy-done.54), channel_id=1, source_target_pairs={{0,8},{2,10},{4,12},{6,14},{8,16},{10,18},{12,20},{14,22},{16,24},... | collective-permute-start | bytes 393224 | tf_op jit(solution)/shard_map/ppermute | solution.py:260
  51.8 23.6 %collective-permute-start.2 = (bf16[64,1024]{1,0:T(8,128)(2,1)S(1)}, bf16[64,1024]{1,0:T(8,128)(2,1)S(1)}, u32[]{:S(2)}, u32[]{:S(2)}) collective-permute-start(bf16[64,1024]{1,0:T(8,128)(2,1)S(1)} %copy-done.54), channel_id=1, source_target_pairs={{0,16},{2,18},{4,20},{6,22},{8,24},{10,26},{12,28},{14,30},{16,0},... | collective-permute-start | bytes 393224 | tf_op jit(solution)/shard_map/ppermute | solution.py:260
  52.5 22.9 %collective-permute-start.3 = (bf16[64,1024]{1,0:T(8,128)(2,1)S(1)}, bf16[64,1024]{1,0:T(8,128)(2,1)S(1)}, u32[]{:S(2)}, u32[]{:S(2)}) collective-permute-start(bf16[64,1024]{1,0:T(8,128)(2,1)S(1)} %copy-done.54), channel_id=1, source_target_pairs={{0,24},{2,26},{4,28},{6,30},{8,0},{10,2},{12,4},{14,6},{16,8},{18,... | collective-permute-start | bytes 393224 | tf_op jit(solution)/shard_map/ppermute | solution.py:260
  76.2 26.1 %collective-permute-start.8 = (bf16[512,1024]{1,0:T(8,128)(2,1)S(1)}, bf16[512,1024]{1,0:T(8,128)(2,1)}, u32[]{:S(2)}, u32[]{:S(2)}) collective-permute-start(bf16[512,1024]{1,0:T(8,128)(2,1)S(1)} %bitcast.155), channel_id=1, source_target_pairs={{1,0},{0,1},{3,2},{2,3},{5,4},{4,5},{7,6},{6,7},{9,8},{8,9},{11,10... | collective-permute-start | bytes 3145736 | tf_op jit(solution)/shard_map/ppermute | solution.py:220
  95.5 24.6 %collective-permute-start.5 = (bf16[8,64,1024]{2,1,0:T(8,128)(2,1)S(1)}, bf16[8,64,1024]{2,1,0:T(8,128)(2,1)}, u32[]{:S(2)}, u32[]{:S(2)}) collective-permute-start(bf16[8,64,1024]{2,1,0:T(8,128)(2,1)S(1)} %bitcast.158), channel_id=1, source_target_pairs={{0,2},{2,0},{4,6},{6,4},{8,10},{10,8},{12,14},{14,12},{16,18},{18,... | collective-permute-start | bytes 3145736 | tf_op jit(solution)/shard_map/ppermute | solution.py:254
  96.4 23.8 %collective-permute-start.6 = (bf16[512,512]{1,0:T(8,128)(2,1)S(1)}, bf16[512,512]{1,0:T(8,128)(2,1)S(1)}, u32[]{:S(2)}, u32[]{:S(2)}) collective-permute-start(bf16[512,512]{1,0:T(8,128)(2,1)S(1)} %copy-done.19), channel_id=1, source_target_pairs={{1,0},{0,1},{3,2},{2,3},{5,4},{4,5},{7,6},{6,7},{9,8},{8,9},{11,10... | collective-permute-start | bytes 1572872 | tf_op jit(solution)/shard_map/ppermute | solution.py:220
  194.0 26.9 %collective-permute-start.10 = (bf16[8,64,2048]{2,1,0:T(8,128)(2,1)}, bf16[8,64,2048]{2,1,0:T(8,128)(2,1)}, u32[]{:S(2)}, u32[]{:S(2)}) collective-permute-start(bf16[8,64,2048]{2,1,0:T(8,128)(2,1)} %get-tuple-element.189), channel_id=1, source_target_pairs={{0,2},{2,0},{4,6},{6,4},{8,10},{10,8},{12,14},{14,12},{16,18},{18,... | collective-permute-start | bytes 6291464 | tf_op jit(solution)/shard_map/ppermute | solution.py:254
  195.3 25.6 %collective-permute-start.9 = (bf16[512,1024]{1,0:T(8,128)(2,1)}, bf16[512,1024]{1,0:T(8,128)(2,1)}, u32[]{:S(2)}, u32[]{:S(2)}) collective-permute-start(bf16[512,1024]{1,0:T(8,128)(2,1)} %get-tuple-element.115), channel_id=1, source_target_pairs={{0,1},{1,0},{2,3},{3,2},{4,5},{5,4},{6,7},{7,6},{8,9},{9,8},{10,11... | collective-permute-start | bytes 3145736 | tf_op jit(solution)/shard_map/ppermute | solution.py:223
  243.2 29.1 %collective-permute-start.13 = (bf16[4,64,2048]{2,1,0:T(8,128)(2,1)}, bf16[4,64,2048]{2,1,0:T(8,128)(2,1)}, u32[]{:S(2)}, u32[]{:S(2)}) collective-permute-start(bf16[4,64,2048]{2,1,0:T(8,128)(2,1)} %get-tuple-element.194), channel_id=1, source_target_pairs={{0,4},{2,6},{4,0},{6,2},{8,12},{10,14},{12,8},{14,10},{16,20},{18,... | collective-permute-start | bytes 3145736 | tf_op jit(solution)/shard_map/ppermute | solution.py:257
  253.3 31.8 %collective-permute-start.14 = (bf16[4,64,1024]{2,1,0:T(8,128)(2,1)S(1)}, bf16[4,64,1024]{2,1,0:T(8,128)(2,1)S(1)}, u32[]{:S(2)}, u32[]{:S(2)}) collective-permute-start(bf16[4,64,1024]{2,1,0:T(8,128)(2,1)S(1)} %get-tuple-element.208), channel_id=1, source_target_pairs={{0,4},{2,6},{4,0},{6,2},{8,12},{10,14},{12,8},{14,10},{16,20},{18,... | collective-permute-start | bytes 1572872 | tf_op jit(solution)/shard_map/ppermute | solution.py:257
  254.0 81.1 %collective-permute-start.23 = (bf16[512,1024]{1,0:T(8,128)(2,1)}, bf16[512,1024]{1,0:T(8,128)(2,1)}, u32[]{:S(2)}, u32[]{:S(2)}) collective-permute-start(bf16[512,1024]{1,0:T(8,128)(2,1)} %get-tuple-element.138), channel_id=1, source_target_pairs={{0,1},{1,0},{2,3},{3,2},{4,5},{5,4},{6,7},{7,6},{8,9},{9,8},{10,11... | collective-permute-start | bytes 3145736 | tf_op jit(solution)/shard_map/ppermute | solution.py:223
  293.2 41.8 %collective-permute-start.17 = (bf16[64,2048]{1,0:T(8,128)(2,1)}, bf16[64,2048]{1,0:T(8,128)(2,1)S(1)}, u32[]{:S(2)}, u32[]{:S(2)}) collective-permute-start(bf16[64,2048]{1,0:T(8,128)(2,1)} %get-tuple-element.206), channel_id=1, source_target_pairs={{0,8},{2,10},{4,12},{6,14},{8,16},{10,18},{12,20},{14,22},{16,24},... | collective-permute-start | bytes 786440 | tf_op jit(solution)/shard_map/ppermute | solution.py:260
  307.3 27.7 %collective-permute-start.18 = (bf16[64,2048]{1,0:T(8,128)(2,1)}, bf16[64,2048]{1,0:T(8,128)(2,1)S(1)}, u32[]{:S(2)}, u32[]{:S(2)}) collective-permute-start(bf16[64,2048]{1,0:T(8,128)(2,1)} %get-tuple-element.205), channel_id=1, source_target_pairs={{0,16},{2,18},{4,20},{6,22},{8,24},{10,26},{12,28},{14,30},{16,0},... | collective-permute-start | bytes 786440 | tf_op jit(solution)/shard_map/ppermute | solution.py:260
  340.6 22.9 %collective-permute-start.24 = (bf16[8,64,768]{2,1,0:T(8,128)(2,1)S(1)}, bf16[8,64,768]{2,1,0:T(8,128)(2,1)}, u32[]{:S(2)}, u32[]{:S(2)}) collective-permute-start(bf16[8,64,768]{2,1,0:T(8,128)(2,1)S(1)} %get-tuple-element.200), channel_id=1, source_target_pairs={{0,2},{2,0},{4,6},{6,4},{8,10},{10,8},{12,14},{14,12},{16,18},{18,... | collective-permute-start | bytes 2359304 | tf_op jit(solution)/shard_map/ppermute | solution.py:254
  351.7 26.9 %collective-permute-start.27 = (bf16[64,768]{1,0:T(8,128)(2,1)}, bf16[64,768]{1,0:T(8,128)(2,1)}, u32[]{:S(2)}, u32[]{:S(2)}) collective-permute-start(bf16[64,768]{1,0:T(8,128)(2,1)} %get-tuple-element.234), channel_id=1, source_target_pairs={{0,8},{2,10},{4,12},{6,14},{8,16},{10,18},{12,20},{14,22},{16,24},... | collective-permute-start | bytes 294920 | tf_op jit(solution)/shard_map/ppermute | solution.py:260
  351.7 26.9 %collective-permute-start.28 = (bf16[64,768]{1,0:T(8,128)(2,1)}, bf16[64,768]{1,0:T(8,128)(2,1)}, u32[]{:S(2)}, u32[]{:S(2)}) collective-permute-start(bf16[64,768]{1,0:T(8,128)(2,1)} %get-tuple-element.233), channel_id=1, source_target_pairs={{0,16},{2,18},{4,20},{6,22},{8,24},{10,26},{12,28},{14,30},{16,0},... | collective-permute-start | bytes 294920 | tf_op jit(solution)/shard_map/ppermute | solution.py:260
  352.3 26.2 %collective-permute-start.29 = (bf16[64,768]{1,0:T(8,128)(2,1)}, bf16[64,768]{1,0:T(8,128)(2,1)}, u32[]{:S(2)}, u32[]{:S(2)}) collective-permute-start(bf16[64,768]{1,0:T(8,128)(2,1)} %get-tuple-element.232), channel_id=1, source_target_pairs={{0,24},{2,26},{4,28},{6,30},{8,0},{10,2},{12,4},{14,6},{16,8},{18,... | collective-permute-start | bytes 294920 | tf_op jit(solution)/shard_map/ppermute | solution.py:260
  373.9 29.2 %collective-permute-start.33 = (bf16[512,1024]{1,0:T(8,128)(2,1)}, bf16[512,1024]{1,0:T(8,128)(2,1)}, u32[]{:S(2)}, u32[]{:S(2)}) collective-permute-start(bf16[512,1024]{1,0:T(8,128)(2,1)} %slice.62), channel_id=1, source_target_pairs={{0,1},{1,0},{2,3},{3,2},{4,5},{5,4},{6,7},{7,6},{8,9},{9,8},{10,11... | collective-permute-start | bytes 3145736 | tf_op jit(solution)/shard_map/ppermute | solution.py:223
  385.6 24.5 %collective-permute-start.30 = (bf16[64,768]{1,0:T(8,128)(2,1)}, bf16[64,768]{1,0:T(8,128)(2,1)}, u32[]{:S(2)}, u32[]{:S(2)}) collective-permute-start(bf16[64,768]{1,0:T(8,128)(2,1)} %get-tuple-element.230), channel_id=1, source_target_pairs={{0,8},{2,10},{4,12},{6,14},{8,16},{10,18},{12,20},{14,22},{16,24},... | collective-permute-start | bytes 294920 | tf_op jit(solution)/shard_map/ppermute | solution.py:260
  387.2 22.8 %collective-permute-start.31 = (bf16[64,768]{1,0:T(8,128)(2,1)}, bf16[64,768]{1,0:T(8,128)(2,1)}, u32[]{:S(2)}, u32[]{:S(2)}) collective-permute-start(bf16[64,768]{1,0:T(8,128)(2,1)} %get-tuple-element.229), channel_id=1, source_target_pairs={{0,16},{2,18},{4,20},{6,22},{8,24},{10,26},{12,28},{14,30},{16,0},... | collective-permute-start | bytes 294920 | tf_op jit(solution)/shard_map/ppermute | solution.py:260
  (89 other events, 1293.0 us)
Sparse Core Ops, SparseCore 0:
  10.9 56.8 all-gather.2
  70.6 75.2 all-gather.4
  208.4 77.2 reduce-scatter.1
